TPU v7x, 32 devices: a whole 2x2x4 slice. The times are simulated.
32 devices in a mesh: seq: 8 (over y, x, core), head: 4 (over z).
Axes of the slice: x: 2, y: 2, z: 4, core: 2. Of those that a mesh axis runs over, the one named last changes fastest.
Arguments:
- tokens: bfloat16 [18432, 1024], P('seq', 'head'), may hold values from -6 to 6
- lengths: int32 [24], replicated, may hold values from 0 to 12288, as said below
- pad_mask: int32 [18432], P('seq'), may hold values 0 or 1
- w_qkv: bfloat16 [3, 1024, 1024], P(None, None, 'head'), may hold values from -0.375 to 0.375
- w_out: bfloat16 [1024, 1024], P('head'), may hold values from -3 to 3
- w_up: bfloat16 [1024, 4096], P(None, 'head'), may hold values from -0.1875 to 0.1875
- w_down: bfloat16 [4096, 1024], P('head'), may hold values from -0.09375 to 0.09375
- norm_gains: float32 [2, 1024], replicated, may hold values from 0.25 to 1.75
- norm_biases: float32 [2, 1024], replicated, may hold values from -1.8 to 1.8
- out_cotangent: bfloat16 [18432, 1024], P('seq', 'head'), may hold values from -6 to 6
Outputs:
- layer_out: bfloat16 [18432, 1024], P('seq', 'head')
- grad_tokens: float32 [18432, 1024], P('seq', 'head')
- grad_w_qkv: float32 [3, 1024, 1024], P(None, 'seq', 'head')
- grad_w_out: float32 [1024, 1024], P('head', 'seq')
- grad_w_up: float32 [1024, 4096], P('seq', 'head')
- grad_w_down: float32 [4096, 1024], P('head', 'seq')
- grad_gains: float32 [2, 1024], P(None, ('head', 'seq'))
- grad_biases: float32 [2, 1024], P(None, ('head', 'seq'))
Inputs may be any that keep to these rules, and one draw needn't show every extreme that they name: Each length is 768, 3072 or 12288 pixels (a 16x16, 32x32 or 64x64 image of three channels), but for the image cut at the end of the packed sequence, which keeps a multiple of 768; the entries after it are 0; the lengths sum to 18432; the first is min(12288, 18432).
All inputs are finite; a program needn't handle non-finite values. No bound on the sum of `pad_mask` on one device may be relied on, other than what follows from the above.
Results may differ from a plain program's by a relative error of at most 0.018.
Values may be sent and summed in bfloat16 or wider, within the bound.
A program may use at most 192 MiB of HBM per device.

v0:
```python
import jax
import jax.numpy as jnp
from jax import lax
from jax.sharding import PartitionSpec as P

HD = 64
BLOCK = 128


highest_matmul_precision = lax.Precision.HIGHEST
norm_eps = 1e-05


def entering(x, axis, combine, identity, reverse):
    count, here = (lax.axis_size(axis), lax.axis_index(axis))
    everything = jax.tree.map(
        lambda part, kind: lax.all_gather(part.astype(kind), axis),
        x,
        jax.tree.map(lambda a: jnp.bfloat16 if a.dtype == jnp.float32 else a.dtype, x),
    )
    start = jax.tree.map(
        lambda part, zero: jnp.broadcast_to(jnp.asarray(zero, part.dtype), part.shape), x, identity
    )

    def lap(k, before):
        at = count - 1 - k if reverse else k
        reached = at > here if reverse else at < here
        new = combine(
            before, jax.tree.map(lambda part, own: part[at].astype(own.dtype), everything, x)
        )
        return jax.tree.map(lambda a, b: jnp.where(reached, a, b), new, before)

    return lax.fori_loop(0, count, lap, start)


def feature_map(values_in):
    return jax.nn.elu(values_in) + 1.0


def layer_norm(rows, gain, bias):
    mean_row = jnp.mean(rows, axis=-1, keepdims=True)
    centered = rows - mean_row
    variance = jnp.mean(centered * centered, axis=-1, keepdims=True)
    return centered * lax.rsqrt(variance + norm_eps) * gain + bias


def block_tables(seg_blocks, seg_before):
    block_count = seg_blocks.shape[0]
    block_width = seg_blocks.shape[1]
    prev_seg = jnp.concatenate([jnp.reshape(seg_before, (1,)), seg_blocks[:-1, -1]])
    cont_mask = (seg_blocks == prev_seg[:, None]).astype(jnp.float32)
    keep_flag = (seg_blocks[:, -1] == prev_seg).astype(jnp.int32)
    open_mask = (seg_blocks == seg_blocks[:, -1:]).astype(jnp.float32)
    causal = jnp.arange(block_width)[:, None] >= jnp.arange(block_width)[None, :]
    same_mask = ((seg_blocks[:, :, None] == seg_blocks[:, None, :]) & causal[None]).astype(
        jnp.float32
    )
    zeros_incl = jnp.cumsum(1 - keep_flag)
    zeros_excl = jnp.concatenate([jnp.zeros((1,), jnp.int32), zeros_incl])
    row_ids = jnp.arange(block_count + 1)[:, None]
    col_ids = jnp.arange(block_count)[None, :]
    carry_blend_term = ((col_ids < row_ids) & (zeros_excl[:, None] == zeros_incl[None, :])).astype(
        jnp.float32
    )
    carry_retain_factor = (zeros_excl == 0).astype(jnp.float32)
    return (cont_mask, open_mask, same_mask, carry_blend_term, carry_retain_factor)


def segment_ids(lengths, positions):
    item_ends = jnp.cumsum(lengths)
    return jnp.sum((positions[:, None] >= item_ends[None, :]).astype(jnp.int32), axis=1)


def link_states(earlier, later):
    return (
        later[2] * earlier[0] + later[0],
        later[2] * earlier[1] + later[1],
        earlier[2] * later[2],
    )


def carry_across(summary, backward):
    identity = (jnp.zeros_like(summary[0]), jnp.zeros_like(summary[1]), jnp.ones((), jnp.float32))
    carried_state, carried_norm, carried_flag = entering(
        summary, "seq", link_states, identity, backward
    )
    return (carried_state, carried_norm)


def norm_back(partial_grad, pullback, head_here, slice_width):
    offset_here = head_here * slice_width
    summed_grad = lax.psum(partial_grad.astype(jnp.bfloat16), "head").astype(jnp.float32)
    d_rows, d_gain, d_bias = pullback(summed_grad)
    return (
        lax.dynamic_slice_in_dim(d_rows, offset_here, slice_width, 1),
        lax.dynamic_slice_in_dim(d_gain, offset_here, slice_width, 0),
        lax.dynamic_slice_in_dim(d_bias, offset_here, slice_width, 0),
    )


def shards(
    tokens, lengths, pad_mask, w_qkv, w_out, w_up, w_down, norm_gains, norm_biases, out_cotangent
):
    row_count = tokens.shape[0]
    slice_width = tokens.shape[1]
    block_count = row_count // BLOCK
    local_heads = w_qkv.shape[2] // HD
    head_here = lax.axis_index("head")
    first_pos = lax.axis_index("seq") * row_count
    positions = first_pos + jnp.arange(row_count, dtype=jnp.int32)
    seg_rows = segment_ids(lengths, positions)
    seg_prior = segment_ids(lengths, jnp.reshape(first_pos - 1, (1,)))[0]
    seg_before = jnp.where(first_pos > 0, seg_prior, -1)
    cont_mask, open_mask, same_mask, carry_blend_term, carry_retain_factor = block_tables(
        seg_rows.reshape(block_count, BLOCK), seg_before
    )
    mask_float = pad_mask.astype(jnp.float32)
    cont_wide = cont_mask[:, :, None, None]
    open_wide = open_mask[:, :, None, None]
    same_low = same_mask.astype(jnp.bfloat16)

    def to_blocks(array_in):
        return array_in.reshape(block_count, BLOCK, local_heads, HD)

    full_rows = lax.all_gather(tokens, "head", axis=1, tiled=True).astype(jnp.float32)
    normed_one, norm_one_pull = jax.vjp(layer_norm, full_rows, norm_gains[0], norm_biases[0])
    normed_one_low = normed_one.astype(jnp.bfloat16)
    projected = jnp.einsum("td,cdh->cth", normed_one_low, w_qkv, preferred_element_type=jnp.float32)
    query_feat, query_pull = jax.vjp(feature_map, projected[0])

    def masked_map(keys_in):
        return mask_float[:, None] * feature_map(keys_in)

    key_feat, key_pull = jax.vjp(masked_map, projected[1])
    feat_q = to_blocks(query_feat.astype(jnp.bfloat16))
    feat_k = to_blocks(key_feat.astype(jnp.bfloat16))
    block_vals = to_blocks(projected[2].astype(jnp.bfloat16))
    feat_q_wide = feat_q.astype(jnp.float32)
    open_keys = feat_k * open_wide.astype(jnp.bfloat16)
    state_additions = jnp.einsum(
        "nuhk,nuhv->nhkv", open_keys, block_vals, preferred_element_type=jnp.float32
    )
    norm_incs = jnp.sum(open_keys.astype(jnp.float32), axis=1)
    self_block_state = jnp.einsum(
        "f,flpi->lpi", carry_blend_term[-1], state_additions, precision=highest_matmul_precision
    )
    own_norm = jnp.einsum(
        "e,ehk->hk", carry_blend_term[-1], norm_incs, precision=highest_matmul_precision
    )
    enter_state, enter_norm = carry_across(
        (self_block_state, own_norm, carry_retain_factor[-1]), False
    )
    block_states = (
        jnp.einsum(
            "me,ehkv->mhkv",
            carry_blend_term[:-1],
            state_additions,
            precision=highest_matmul_precision,
        )
        + carry_retain_factor[:-1, None, None, None] * enter_state[None]
    )
    block_norms = (
        jnp.einsum(
            "me,ehk->mhk", carry_blend_term[:-1], norm_incs, precision=highest_matmul_precision
        )
        + carry_retain_factor[:-1, None, None] * enter_norm[None]
    )
    states_low = block_states.astype(jnp.bfloat16)
    scores_low = (
        same_mask[:, None]
        * jnp.einsum("nthk,nuhk->nhtu", feat_q, feat_k, preferred_element_type=jnp.float32)
    ).astype(jnp.bfloat16)
    numer = jnp.einsum(
        "nhtu,nuhv->nthv", scores_low, block_vals, preferred_element_type=jnp.float32
    ) + cont_wide * jnp.einsum(
        "nthk,nhkv->nthv", feat_q, states_low, preferred_element_type=jnp.float32
    )
    key_sums = (
        jnp.einsum("ntu,nuhk->nthk", same_low, feat_k, preferred_element_type=jnp.float32)
        + cont_wide * block_norms[:, None]
    )
    denom = 1.0 + jnp.sum(feat_q_wide * key_sums, axis=-1)
    attended = (numer / denom[..., None]).reshape(row_count, local_heads * HD).astype(jnp.bfloat16)
    attn_terms = jnp.dot(attended, w_out, preferred_element_type=jnp.float32)
    attn_part = lax.psum_scatter(attn_terms, "head", scatter_dimension=1, tiled=True)
    middle = tokens.astype(jnp.float32) + attn_part
    middle_full = lax.all_gather(middle, "head", axis=1, tiled=True)
    normed_two, norm_two_pull = jax.vjp(layer_norm, middle_full, norm_gains[1], norm_biases[1])
    normed_two_low = normed_two.astype(jnp.bfloat16)
    up_pre = jnp.dot(normed_two_low, w_up, preferred_element_type=jnp.float32)
    gelu_val, gelu_pull = jax.vjp(jax.nn.gelu, up_pre)
    hidden_low = gelu_val.astype(jnp.bfloat16)
    mlp_terms = jnp.dot(hidden_low, w_down, preferred_element_type=jnp.float32)
    layer_out = (
        middle
        + lax.psum_scatter(
            mlp_terms.astype(jnp.bfloat16), "head", scatter_dimension=1, tiled=True
        ).astype(jnp.float32)
    ).astype(jnp.bfloat16)
    cot_full = lax.all_gather(out_cotangent, "head", axis=1, tiled=True)
    grad_down = jnp.einsum("tf,td->fd", hidden_low, cot_full, preferred_element_type=jnp.float32)
    d_hidden = jnp.einsum("td,fd->tf", cot_full, w_down, preferred_element_type=jnp.float32)
    up_grad = gelu_pull(d_hidden)[0].astype(jnp.bfloat16)
    grad_up = jnp.einsum("td,tf->df", normed_two_low, up_grad, preferred_element_type=jnp.float32)
    d_norm_two = jnp.einsum("tf,df->td", up_grad, w_up, preferred_element_type=jnp.float32)
    d_mid_norm, gain_two, bias_two = norm_back(d_norm_two, norm_two_pull, head_here, slice_width)
    d_middle = out_cotangent.astype(jnp.float32) + d_mid_norm
    back_full = lax.all_gather(d_middle.astype(jnp.bfloat16), "head", axis=1, tiled=True)
    grad_out_w = jnp.einsum("tf,td->fd", attended, back_full, preferred_element_type=jnp.float32)
    d_attended = jnp.einsum("td,fd->tf", back_full, w_out, preferred_element_type=jnp.float32)
    d_mixed = to_blocks(d_attended)
    d_numer_low = (d_mixed / denom[..., None]).astype(jnp.bfloat16)
    d_denom = -jnp.sum(d_mixed * numer, axis=-1) / (denom * denom)
    d_feat_q = d_denom[..., None] * key_sums
    d_key_sums = d_denom[..., None] * feat_q_wide
    d_feat_k = jnp.einsum(
        "ntu,nthk->nuhk", same_mask, d_key_sums, precision=highest_matmul_precision
    )
    d_block_norms = jnp.sum(cont_wide * d_key_sums, axis=1)
    cont_numer = d_numer_low * cont_wide.astype(jnp.bfloat16)
    d_feat_q = d_feat_q + jnp.einsum(
        "nthv,nhkv->nthk", cont_numer, states_low, preferred_element_type=jnp.float32
    )
    block_state_gradient = jnp.einsum(
        "nthk,nthv->nhkv", feat_q, cont_numer, preferred_element_type=jnp.float32
    )
    d_scores_low = (
        same_mask[:, None]
        * jnp.einsum("nthv,nuhv->nhtu", d_numer_low, block_vals, preferred_element_type=jnp.float32)
    ).astype(jnp.bfloat16)
    d_feat_q = d_feat_q + jnp.einsum(
        "nhtu,nuhk->nthk", d_scores_low, feat_k, preferred_element_type=jnp.float32
    )
    d_feat_k = d_feat_k + jnp.einsum(
        "nhtu,nthk->nuhk", d_scores_low, feat_q, preferred_element_type=jnp.float32
    )
    d_block_vals = jnp.einsum(
        "nhtu,nthv->nuhv", scores_low, d_numer_low, preferred_element_type=jnp.float32
    )
    self_block_backward = jnp.einsum(
        "t,tpyr->pyr",
        carry_retain_factor[:-1],
        block_state_gradient,
        precision=highest_matmul_precision,
    )
    own_back_norm = jnp.einsum(
        "m,mhk->hk", carry_retain_factor[:-1], d_block_norms, precision=highest_matmul_precision
    )
    exit_state, exit_norm = carry_across(
        (self_block_backward, own_back_norm, carry_retain_factor[-1]), True
    )
    d_incs_low = (
        jnp.einsum(
            "me,mhkv->ehkv",
            carry_blend_term[:-1],
            block_state_gradient,
            precision=highest_matmul_precision,
        )
        + carry_blend_term[-1][:, None, None, None] * exit_state[None]
    ).astype(jnp.bfloat16)
    d_norm_incs = (
        jnp.einsum(
            "me,mhk->ehk", carry_blend_term[:-1], d_block_norms, precision=highest_matmul_precision
        )
        + carry_blend_term[-1][:, None, None] * exit_norm[None]
    )
    d_feat_k = d_feat_k + open_wide * (
        jnp.einsum("nuhv,nhkv->nuhk", block_vals, d_incs_low, preferred_element_type=jnp.float32)
        + d_norm_incs[:, None]
    )
    d_block_vals = d_block_vals + jnp.einsum(
        "nuhk,nhkv->nuhv", open_keys, d_incs_low, preferred_element_type=jnp.float32
    )
    flat_width = local_heads * HD
    d_queries = query_pull(d_feat_q.reshape(row_count, flat_width))[0]
    d_keys = key_pull(d_feat_k.reshape(row_count, flat_width))[0]
    d_projected = jnp.stack(
        [d_queries, d_keys, d_block_vals.reshape(row_count, flat_width)]
    ).astype(jnp.bfloat16)
    grad_qkv = jnp.einsum(
        "td,cth->cdh", normed_one_low, d_projected, preferred_element_type=jnp.float32
    )
    d_norm_one = jnp.einsum("cth,cdh->td", d_projected, w_qkv, preferred_element_type=jnp.float32)
    d_in_norm, gain_one, bias_one = norm_back(d_norm_one, norm_one_pull, head_here, slice_width)
    grad_tokens = d_middle + d_in_norm
    gain_grads = jnp.stack([gain_one, gain_two])
    bias_grads = jnp.stack([bias_one, bias_two])
    summed = (
        lax.psum_scatter(
            grad_qkv.astype(jnp.bfloat16), "seq", scatter_dimension=1, tiled=True
        ).astype(jnp.float32),
        lax.psum_scatter(
            grad_out_w.astype(jnp.bfloat16), "seq", scatter_dimension=1, tiled=True
        ).astype(jnp.float32),
        lax.psum_scatter(
            grad_up.astype(jnp.bfloat16), "seq", scatter_dimension=0, tiled=True
        ).astype(jnp.float32),
        lax.psum_scatter(
            grad_down.astype(jnp.bfloat16), "seq", scatter_dimension=1, tiled=True
        ).astype(jnp.float32),
        lax.psum_scatter(
            gain_grads.astype(jnp.bfloat16), "seq", scatter_dimension=1, tiled=True
        ).astype(jnp.float32),
        lax.psum_scatter(
            bias_grads.astype(jnp.bfloat16), "seq", scatter_dimension=1, tiled=True
        ).astype(jnp.float32),
    )
    return (
        layer_out,
        grad_tokens,
        summed[0],
        summed[1],
        summed[2],
        summed[3],
        summed[4],
        summed[5],
    )


def solution(mesh):
    in_specs = (
        P("seq", "head"),
        P(),
        P("seq"),
        P(None, None, "head"),
        P("head", None),
        P(None, "head"),
        P("head", None),
        P(),
        P(),
        P("seq", "head"),
    )
    out_specs = (
        P("seq", "head"),
        P("seq", "head"),
        P(None, "seq", "head"),
        P("head", "seq"),
        P("seq", "head"),
        P("head", "seq"),
        P(None, ("head", "seq")),
        P(None, ("head", "seq")),
    )
    return jax.shard_map(shards, mesh=mesh, in_specs=in_specs, out_specs=out_specs, check_vma=False)
```

profile of v0, /device:TPU:24, one launch (start us, length us, event | category | flops | bytes accessed | tf_op | source)
XLA Modules:
  0.0 1467.8 jit_solution(3945924201759089983)
XLA Ops:
  14.0 14.1 all-reduce
  33.2 63.6 %all-gather.11.cloned.1.call-done = bf16[2304,1024]{1,0:T(8,128)(2,1)} async-done(((bf16[2304,256]{1,0:T(8,128)(2,1)}), bf16[2304,1024]{1,0:T(8,128)(2,1)}) %all-gather.11.cloned.1.call-update) | async-done | bytes 4718608 | tf_op jit(solution)/shard_map/all_gather | solution.py:125
  96.9 3.2 convert_reduce_fusion.2
  102.1 4.8 convolution_bitcast_fusion
  114.8 4.6 copy.177
  119.4 5.3 reshape.409
  124.7 5.8 copy.170
  130.5 5.3 reshape.410
  135.7 5.8 copy.174
  141.5 3.1 convert_reduce_fusion.3
  144.7 9.2 all-gather.4
  156.1 3.9 fusion.31
  160.0 10.8 all-gather
  170.8 17.6 %while.34 = (s32[]{:T(128)}, f32[4,64,64]{2,1,0:T(8,128)S(1)}, f32[4,64]{1,0:T(4,128)S(1)}, s32[]{:T(128)}, bf16[8]{0:T(256)(128)(2,1)S(1)}, /*index=5*/bf16[8,4...) while((s32[]{:T(128)}, f32[4,64,64]{2,1,0:T(8,128)S(1)}, ...), condition=%wide.region_8.9_spmd.clone, body=%wide.region_7.8_spmd.clone.sunk | while | flops 83205 | bytes 166553 | solution.py:33
  188.4 4.8 add_convert_fusion.2
  199.5 3.2 fusion.45
  204.7 5.1 fusion.57
  210.6 160.3 %reduce-scatter.19.cloned.1.call-done = f32[2304,256]{1,0:T(8,128)} async-done(((f32[2304,1024]{1,0:T(8,128)}), f32[2304,256]{1,0:T(8,128)}) %reduce-scatter.19.cloned.1.call-update) | async-done | bytes 2359312 | tf_op jit(solution)/shard_map/reduce_scatter | solution.py:185
  370.9 3.6 convert_add_fusion.4
  374.8 85.3 %all-gather.15.cloned.1.call-done = bf16[2304,1024]{1,0:T(8,128)(2,1)} async-done(((bf16[2304,256]{1,0:T(8,128)(2,1)}), bf16[2304,1024]{1,0:T(8,128)(2,1)}) %all-gather.15.cloned.1.call-update) | async-done | bytes 4718608 | tf_op jit(solution)/shard_map/all_gather | solution.py:200
  460.1 10.2 fusion.122
  470.3 156.0 %all-gather.13.cloned.1.call-done = f32[2304,1024]{1,0:T(8,128)} async-done(((f32[2304,256]{1,0:T(8,128)}), f32[2304,1024]{1,0:T(8,128)}) %all-gather.13.cloned.1.call-update) | async-done | bytes 9437200 | tf_op jit(solution)/shard_map/all_gather | solution.py:187
  626.3 4.2 reduce_sum.168
  630.5 4.9 multiply_reduce_fusion
  638.6 15.6 %fusion.23 = (bf16[2304,1024]{1,0:T(8,128)(2,1)S(1)}, f32[2304,1024]{1,0:T(8,128)}) fusion(f32[2304,1024]{1,0:T(8,128)} %fusion.122, bf16[2304,1024]{1,0:T(8,128)(2,1)S(1)} %add_convert_fusion, bf16[1024,1024]{1,0:T(8,128)(2,1)S(1)} %copy-done), kind=kOutput, calls=%fused_computation.39 | convolution fusion | flops 4879024128 | bytes 30408704 | tf_op jit(solution)/shard_map/dot_general | solution.py:190
  656.4 6.8 convolution_convert_fusion
  663.4 170.8 %all-reduce.4.cloned.1.call-done = bf16[2304,1024]{1,0:T(8,128)(2,1)} async-done(((bf16[2304,1024]{1,0:T(8,128)(2,1)}), bf16[2304,1024]{1,0:T(8,128)(2,1)}) %all-reduce.4.cloned.1.call-update) | async-done | bytes 4718608 | tf_op jit(solution)/shard_map/psum | solution.py:92
  834.3 7.6 fusion.24
  841.9 6.5 fusion.113
  848.4 3.6 copy-done.10
  853.5 9.3 convolution_convert_fusion.2
  865.5 9.5 convolution_convert_fusion.3
  875.1 10.5 convolution_convert_fusion.1
  886.1 55.1 %all-gather.17.cloned.1.call-done = bf16[2304,1024]{1,0:T(8,128)(2,1)} async-done(((bf16[2304,256]{1,0:T(8,128)(2,1)}), bf16[2304,1024]{1,0:T(8,128)(2,1)}) %all-gather.17.cloned.1.call-update) | async-done | bytes 4718608 | tf_op jit(solution)/shard_map/all_gather | solution.py:208
  941.2 4.5 convolution_convert_fusion.5
  947.7 5.4 fusion.123
  953.1 3.7 reshape.348
  956.8 3.7 fusion.46
  962.8 3.9 fusion.27
  968.9 8.9 all-gather.5
  977.7 11.3 all-gather.2
  989.1 17.8 %while.35 = (s32[]{:T(128)}, f32[4,64,64]{2,1,0:T(8,128)S(1)}, f32[4,64]{1,0:T(4,128)S(1)}, s32[]{:T(128)}, bf16[8]{0:T(256)(128)(2,1)S(1)}, /*index=5*/bf16[8,4...) while((s32[]{:T(128)}, f32[4,64,64]{2,1,0:T(8,128)S(1)}, ...), condition=%wide.region_20.21_spmd.clone, body=%wide.region_19.20_spmd.clone.sunk | while | flops 83209 | bytes 166615 | solution.py:33
  1006.9 5.9 add_convert_fusion.1
  1019.9 4.7 copy.220
  1024.6 4.6 reshape.397
  1029.2 3.1 fusion.59
  1037.7 5.5 copy.219
  1043.2 5.5 reshape.396
  1054.6 5.5 copy.237
  1060.0 5.7 reshape.411
  1065.9 4.8 add_convert_fusion.5
  1072.1 5.7 fusion.51
  1077.9 2.9 copy.221
  1082.4 8.1 bitcast_convert_fusion
  1094.8 24.9 %reduce-scatter.21.cloned.1.call-done = bf16[2304,256]{1,0:T(8,128)(2,1)} async-done(((bf16[2304,1024]{1,0:T(8,128)(2,1)}), bf16[2304,256]{1,0:T(8,128)(2,1)}) %reduce-scatter.21.cloned.1.call-update) | async-done | bytes 1179664 | tf_op jit(solution)/shard_map/reduce_scatter | solution.py:196
  1119.7 3.3 add_convert_fusion.6
  1123.0 35.1 %reduce-scatter.27.cloned.1.call-done = bf16[128,256]{1,0:T(8,128)(2,1)} async-done(((bf16[1024,256]{1,0:T(8,128)(2,1)}), bf16[128,256]{1,0:T(8,128)(2,1)}) %reduce-scatter.27.cloned.1.call-update) | async-done | bytes 65552
  1159.7 41.1 %reduce-scatter.25.cloned.1.call-done = bf16[128,768]{1,0:T(8,128)(2,1)} async-done(((bf16[1024,768]{1,0:T(8,128)(2,1)}), bf16[128,768]{1,0:T(8,128)(2,1)}) %reduce-scatter.25.cloned.1.call-update) | async-done | bytes 196624
  1202.9 169.9 %all-reduce.6.cloned.1.call-done = bf16[2304,1024]{1,0:T(8,128)(2,1)} async-done(((bf16[2304,1024]{1,0:T(8,128)(2,1)}), bf16[2304,1024]{1,0:T(8,128)(2,1)}) %all-reduce.6.cloned.1.call-update) | async-done | bytes 4718608 | tf_op jit(solution)/shard_map/psum | solution.py:92
  1372.8 6.5 fusion.25
  1379.5 8.4 fusion.111
  1389.6 4.2 fusion.43
  1393.8 29.6 %reduce-scatter.31.cloned.1.call-done = bf16[32,2]{1,0:T(8,128)(2,1)} async-done(((bf16[256,2]{1,0:T(8,128)(2,1)}), bf16[32,2]{1,0:T(8,128)(2,1)}) %reduce-scatter.31.cloned.1.call-update) | async-done | bytes 144
  1424.8 34.8 %reduce-scatter.33.cloned.1.call-done = bf16[32,2]{1,0:T(8,128)(2,1)} async-done(((bf16[256,2]{1,0:T(8,128)(2,1)}), bf16[32,2]{1,0:T(8,128)(2,1)}) %reduce-scatter.33.cloned.1.call-update) | async-done | bytes 144
  (291 shorter events, 107.3 us)
Async XLA Ops:
  7.2 631.4 %copy-start = (bf16[1024,1024]{1,0:T(8,128)(2,1)S(1)}, bf16[1024,1024]{1,0:T(8,128)(2,1)}, u32[]{:S(2)}) copy-start(bf16[1024,1024]{1,0:T(8,128)(2,1)} %param.19) | copy-start | bytes 6291460
  7.2 89.7 %all-gather.11.cloned.1.call-start = ((), (), s32[]{:S(2)}) async-start(), calls=%async_computation.8 | async-start | bytes 5898240 | tf_op jit(solution)/shard_map/all_gather | solution.py:125
  7.9 363.0 %reduce-scatter.19.cloned.1.call-start = ((), (), s32[]{:S(2)}) async-start(), calls=%async_computation.9 | async-start | bytes 11796480 | tf_op jit(solution)/shard_map/reduce_scatter | solution.py:185
  10.8 86.1 %copy-start.50 = (pred[19]{0:T(512)(128)(4,1)}, pred[19]{0:T(512)(128)(4,1)S(1)}, u32[]{:S(2)}) copy-start(pred[19]{0:T(512)(128)(4,1)S(1)} %get-tuple-element.447) | copy-start | bytes 61
  29.1 72.9 %copy-start.48 = (f32[1,1024]{1,0:T(1,128)}, f32[1,1024]{1,0:T(1,128)S(1)}, u32[]{:S(2)}) copy-start(f32[1,1024]{1,0:T(1,128)S(1)} %get-tuple-element.469) | copy-start | bytes 12292
  29.9 72.1 %copy-start.52 = (f32[1,1024]{1,0:T(1,128)}, f32[1,1024]{1,0:T(1,128)S(1)}, u32[]{:S(2)}) copy-start(f32[1,1024]{1,0:T(1,128)S(1)} %get-tuple-element.471) | copy-start | bytes 12292
  96.9 3.8 copy-start.3
  102.0 4.9 copy-start.43
  102.0 4.9 copy-start.41
  106.9 2.9 copy-start.18
  141.5 12.4 copy-start.13
  188.4 5.0 copy-start.28
  193.2 4.1 copy-start.24
  193.4 3.0 copy-start.37
  193.4 3.0 copy-start.22
  197.4 2.1 copy-start.14
  202.7 2.0 copy-start.36
  209.8 250.3 %all-gather.15.cloned.1.call-start = ((), (), s32[]{:S(2)}) async-start(), calls=%async_computation.12 | async-start | bytes 5898240 | tf_op jit(solution)/shard_map/all_gather | solution.py:200
  210.5 415.8 %all-gather.13.cloned.1.call-start = ((), (), s32[]{:S(2)}) async-start(), calls=%async_computation.10 | async-start | bytes 11796480 | tf_op jit(solution)/shard_map/all_gather | solution.py:187
  374.6 459.7 %all-reduce.4.cloned.1.call-start = ((), (), s32[]{:S(2)}) async-start(), calls=%async_computation.13 | async-start | bytes 9437184 | tf_op jit(solution)/shard_map/psum | solution.py:92
  630.5 6.4 copy-start.2
  638.6 15.6 %copy-start.31 = (bf16[2304,1024]{1,0:T(8,128)(2,1)}, bf16[2304,1024]{1,0:T(8,128)(2,1)S(1)}, u32[]{:S(2)}) copy-start(bf16[2304,1024]{1,0:T(8,128)(2,1)S(1)} %add_convert_fusion) | copy-start | bytes 14155780
  654.2 2.1 copy-start.55
  663.2 278.0 %all-gather.17.cloned.1.call-start = ((), (), s32[]{:S(2)}) async-start(), calls=%async_computation.14 | async-start | bytes 5898240 | tf_op jit(solution)/shard_map/all_gather | solution.py:208
  834.3 7.6 copy-start.16
  841.9 10.1 copy-start.20
  848.4 3.7 copy-start.10
  853.5 237.4 %reduce-scatter.29.cloned.1.call-start = ((), (), s32[]{:S(2)}) async-start(), calls=%async_computation.19 | async-start | bytes 2359296
  865.4 227.4 %reduce-scatter.23.cloned.1.call-start = ((), (), s32[]{:S(2)}) async-start(), calls=%async_computation.16 | async-start | bytes 2359296 | tf_op jit(solution)/shard_map/reduce_scatter | solution.py:295
  875.0 244.7 %reduce-scatter.21.cloned.1.call-start = ((), (), s32[]{:S(2)}) async-start(), calls=%async_computation.11 | async-start | bytes 5898240 | tf_op jit(solution)/shard_map/reduce_scatter | solution.py:196
  885.6 55.6 %copy-start.30 = (bf16[18,128,4,64]{1,0,3,2:T(8,128)(2,1)S(1)}, bf16[18,128,4,64]{1,0,3,2:T(8,128)(2,1)}, u32[]{:S(2)}) copy-start(bf16[18,128,4,64]{1,0,3,2:T(8,128)(2,1)} %copy-done.29) | copy-start | bytes 3538948
  885.6 272.4 %reduce-scatter.27.cloned.1.call-start = ((), (), s32[]{:S(2)}) async-start(), calls=%async_computation.18 | async-start | bytes 589824
  956.8 3.7 copy-start.5
  956.8 3.7 copy-start.45
  960.5 2.3 copy-start.6
  960.5 2.2 copy-start.51
  1015.7 1.9 copy-start.7
  1015.7 2.4 copy-start.27
  1029.2 3.1 copy-start.8
  1029.2 3.1 copy-start.15
  1029.2 3.1 copy-start.23
  1033.3 2.1 copy-start.19
  1033.3 2.1 copy-start.47
  1043.2 5.5 copy-start.9
  1043.2 7.6 copy-start.38
  1048.7 2.2 copy-start.12
  1048.7 3.0 copy-start.25
  1060.0 5.7 copy-start.46
  1060.0 12.0 slice-start
  1065.7 135.0 %reduce-scatter.25.cloned.1.call-start = ((), (), s32[]{:S(2)}) async-start(), calls=%async_computation.17 | async-start | bytes 1769472
  1065.8 6.3 slice-start.1
  1065.8 6.3 copy-start.35
  1065.8 6.3 copy-start.40
  1065.8 6.3 copy-start.42
  1065.8 6.3 copy-start.49
  1065.8 6.3 copy-start.53
  1080.8 1.6 copy-start.33
  1082.4 290.4 %all-reduce.6.cloned.1.call-start = ((), (), s32[]{:S(2)}) async-start(), calls=%async_computation.15 | async-start | bytes 9437184 | tf_op jit(solution)/shard_map/psum | solution.py:92
  1090.6 332.8 %reduce-scatter.31.cloned.1.call-start = ((), (), s32[]{:S(2)}) async-start(), calls=%async_computation.20 | async-start | bytes 73728
  1202.9 176.6 %copy-start.44 = (f32[2304]{0:T(1024)S(1)}, f32[2304]{0:T(1024)}, u32[]{:S(2)}) copy-start(f32[2304]{0:T(1024)} %copy-done.43) | copy-start | bytes 27652
  1372.8 6.6 copy-start.17
  1379.4 10.2 copy-start.21
  1388.8 70.7 %reduce-scatter.33.cloned.1.call-start = ((), (), s32[]{:S(2)}) async-start(), calls=%async_computation.21 | async-start | bytes 73728
  1389.6 71.3 %copy-start.1 = (bf16[1024,1024]{1,0:T(8,128)(2,1)S(1)}, bf16[1024,1024]{1,0:T(8,128)(2,1)}, u32[]{:S(2)}) copy-start(bf16[1024,1024]{1,0:T(8,128)(2,1)} %param.19) | copy-start | bytes 6291460
  (8 other events, 10.4 us)
Sparse Core Ops, SparseCore 0:
  9.6 87.2 all-gather.10
  209.9 160.9 reduce-scatter.18
  372.5 87.5 all-gather.14
  461.5 164.7 all-gather.12
  663.3 170.9 all-reduce.3
  853.6 87.5 all-gather.16
  944.4 42.6 reduce-scatter.28
  990.8 41.9 reduce-scatter.22
  1035.1 84.5 reduce-scatter.20
  1122.6 35.3 reduce-scatter.26
  1162.3 38.4 reduce-scatter.24
  1203.1 169.6 all-reduce.5
  1388.9 34.4 reduce-scatter.30
  1426.3 33.2 reduce-scatter.32
where the time goes:
time: 1480 us; the launch traced here: 1470 us
  waiting for transfers between devices  1030 us (70%)
  matrix products  142 us (10%)
  local copies, waits for them, and re-layouts  120 us (8%)
  other arithmetic  94.6 us (6%)
  blocking collectives  54.3 us (4%)
  between operations  15.9 us (1%)
    psum x2, waiting for transfers between devices, norm_back(): lax.psum(partial_grad.astype(jnp.bfloat16), 'head').astype(jnp.float32)  341 us
    reduce_scatter x1, waiting for transfers between devices, shards(): lax.psum_scatter(attn_terms, 'head', scatter_dimension=1, tiled=True)  160 us
    all_gather x1, waiting for transfers between devices, shards(): middle_full = lax.all_gather(middle, 'head', axis=1, tiled=True)  156 us
    unnamed x19, waiting for transfers between devices  142 us
    all_gather x1, waiting for transfers between devices, shards(): cot_full = lax.all_gather(out_cotangent, 'head', axis=1, tiled=True)  85.3 us
    all_gather x1, waiting for transfers between devices, shards(): lax.all_gather(tokens, 'head', axis=1, tiled=True).astype(jnp.float32)  63.6 us
    all_gather x1, waiting for transfers between devices, shards(): lax.all_gather(d_middle.astype(jnp.bfloat16), 'head', axis=1, tiled=True)  55.1 us
    all_gather x4, blocking collectives, entering(): lax.all_gather(part.astype(kind), axis)  40.2 us
  transfers between devices with their start and end apart: 14, of which 12 were waited for; matrix products, arithmetic and copies ran while one was open for 13% of the time, Pallas kernels for 0%

commit v1 on v0

v1 whole, which is shorter than its diff:
```python
import functools
import math

import jax
import jax.numpy as jnp
from jax import lax
from jax.experimental import pallas as pl
from jax.experimental.pallas import tpu as pltpu
from jax.sharding import PartitionSpec as P

HD = 64
UNIT = 768
EPS = 1e-05
MESH = pl.DeviceIdType.MESH
BF = jnp.bfloat16
F32 = jnp.float32
MSG = 80


def bit_orders(ns):
    m = ns.bit_length() - 1
    xs = list(range(1, 1 + (m - 1) // 2))
    ys = list(range(1 + (m - 1) // 2, m))
    return xs + ys, ys + xs


def bits_to(s, order):
    out = 0
    for j, b in enumerate(order):
        out = out + (((s >> b) & 1) << j)
    return out


def rcopy(src, dst, send, recv, dev):
    return pltpu.make_async_remote_copy(
        src_ref=src, dst_ref=dst, send_sem=send, recv_sem=recv, device_id=dev, device_id_type=MESH
    )


def enter(devs):
    bar = pltpu.get_barrier_semaphore()
    for d in devs:
        pl.semaphore_signal(bar, inc=1, device_id=d, device_id_type=MESH)
    pl.semaphore_wait(bar, len(devs))


def z_others(s, h, nz):
    return [(s, lax.rem(h + d, nz)) for d in range(1, nz)]


def run_waves(groups):
    live = []
    pending = list(groups)
    while pending or live:
        if pending:
            live.append(pending.pop(0))
        nxt = []
        for group in live:
            kept = []
            for gen in group:
                try:
                    next(gen)
                    kept.append(gen)
                except StopIteration:
                    pass
            if kept:
                nxt.append(kept)
        live = nxt


def gather_kernel(ns, nz, tok, cot, w4, wu, wd, x, co, w4g, wug, wdg, lsem, tsend, trecv, zsend, zrecv, psend, precv):
    s, h = lax.axis_index("seq"), lax.axis_index("head")
    o0, o1 = bit_orders(ns)
    orders = (o0 + [0], o1 + [0])
    m = len(orders[0])
    t = x.shape[0]
    ew = tok.shape[1]
    arrays = ((w4, w4g), (wu, wug), (wd, wdg))
    half = w4.shape[1] // 2
    r = half // ns
    zdev = z_others(s, h, nz)
    enter(zdev + [(jnp.bitwise_xor(s, 1 << b), h) for b in orders[0]])
    sends = []
    local = []

    def a2a(i, src, dst):
        for d, dev in enumerate(zdev):
            cp = rcopy(
                src.at[pl.ds(dev[1] * t, t), :],
                dst.at[:, pl.ds(h * ew, ew)],
                tsend.at[i * (nz - 1) + d],
                trecv.at[i * (nz - 1) + d],
                dev,
            )
            cp.start()
            sends.append((None, cp))
        lc = pltpu.make_async_copy(src.at[pl.ds(h * t, t), :], dst.at[:, pl.ds(h * ew, ew)], lsem.at[i])
        lc.start()
        local.append(lc)

    def a2a_wait(i, src, dst):
        for d in range(nz - 1):
            frm = lax.rem(h + nz - 1 - d, nz)
            rcopy(
                src.at[pl.ds(h * t, t), :],
                dst.at[:, pl.ds(frm * ew, ew)],
                tsend.at[i * (nz - 1) + d],
                trecv.at[i * (nz - 1) + d],
                (s, frm),
            ).wait_recv()

    pos = [bits_to(s, order) for order in orders]

    def zsem(a, f, k, d):
        return ((a * 2 + f) * (nz - 1) + k) * 2 + d

    def zcopy(a, f, k, d, origin, own):
        w, wg = arrays[a]
        rows = pl.ds(f * half + pos[f] * r, r)
        dst = wg.at[origin, :, rows, :]
        src = w.at[:, rows, :] if own else dst
        i = zsem(a, f, k, d)
        return rcopy(src, dst, zsend.at[i], zrecv.at[i], (s, h + 1 if d == 0 else h - 1))

    def zstart(a, f, k, d, origin, cond):
        cp = zcopy(a, f, k, d, origin, k == 0)
        pl.when(cond)(cp.start)
        sends.append((cond, cp))

    def piece(a, f, k, d):
        wg = arrays[a][1]
        origin = h - 1 - k if d == 0 else h + 1 + k
        valid = origin >= 0 if d == 0 else origin < nz
        pl.when(valid)(zcopy(a, f, k, d, origin, False).wait_recv)
        if k + 1 < nz - 1:
            more = valid & ((h + 1 < nz) if d == 0 else (h >= 1))
            zstart(a, f, k + 1, d, origin, more)
        for j, b in enumerate(orders[f]):
            n = r << j
            begin = (pos[f] >> j) << j
            other = jnp.bitwise_xor(begin, 1 << j)
            i = zsem(a, f, k, d) * m + j
            dev = (jnp.bitwise_xor(s, 1 << b), h)
            mine = wg.at[origin, :, pl.ds(f * half + begin * r, n), :]
            theirs = wg.at[origin, :, pl.ds(f * half + other * r, n), :]
            out = rcopy(mine, mine, psend.at[i], precv.at[i], dev)
            pl.when(valid)(out.start)
            sends.append((valid, out))
            yield
            pl.when(valid)(rcopy(theirs, theirs, psend.at[i], precv.at[i], dev).wait_recv)

    a2a(0, tok, x)
    for a in range(3):
        for f in range(2):
            zstart(a, f, 0, 0, h, h + 1 < nz)
            zstart(a, f, 0, 1, h, h >= 1)
        if a == 0:
            a2a(1, cot, co)
    for a, (w, wg) in enumerate(arrays):
        lc = pltpu.make_async_copy(w, wg.at[h], lsem.at[2 + a])
        lc.start()
        local.append(lc)
    groups = [[piece(a, f, k, d) for d in range(2) for f in range(2)] for a in range(3) for k in range(nz - 1)]
    run_waves(groups)
    a2a_wait(0, tok, x)
    a2a_wait(1, cot, co)
    for lc in local:
        lc.wait()
    for cond, cp in sends:
        if cond is None:
            cp.wait_send()
        else:
            pl.when(cond)(cp.wait_send)


def any_spec():
    return pl.BlockSpec(memory_space=pl.ANY)


def vmem_spec():
    return pl.BlockSpec(memory_space=pltpu.VMEM)


def smem_spec():
    return pl.BlockSpec(memory_space=pltpu.SMEM)


def gather_all(ns, nz, tok, cot, w4, wu, wd):
    t, d = tok.shape[0] // nz, w4.shape[1]
    m = ns.bit_length() - 1
    nzs = 3 * 2 * (nz - 1) * 2
    dma = pltpu.SemaphoreType.DMA
    return pl.pallas_call(
        functools.partial(gather_kernel, ns, nz),
        out_shape=(
            jax.ShapeDtypeStruct((t, d), BF),
            jax.ShapeDtypeStruct((t, d), BF),
            jax.ShapeDtypeStruct((nz,) + w4.shape, BF),
            jax.ShapeDtypeStruct((nz,) + wu.shape, BF),
            jax.ShapeDtypeStruct((nz,) + wd.shape, BF),
        ),
        in_specs=[any_spec()] * 5,
        out_specs=(any_spec(),) * 5,
        scratch_shapes=[
            dma((5,)),
            dma((2 * (nz - 1),)),
            dma((2 * (nz - 1),)),
            dma((nzs,)),
            dma((nzs,)),
            dma((nzs * m,)),
            dma((nzs * m,)),
        ],
        name="gather_all",
        compiler_params=pltpu.CompilerParams(collective_id=0, has_side_effects=True),
    )(tok, cot, w4, wu, wd)


def scan_kernel(ns, nz, wt, wp, wl, msg, out, r1, r2, tot, outb, s1, q1, s2, q2, s3, q3):
    s, h = lax.axis_index("seq"), lax.axis_index("head")
    zdev = z_others(s, h, nz)
    sdev = [(jnp.bitwise_xor(s, d), h) for d in range(1, ns)]
    enter(zdev + sdev)
    sends = []
    for d, dev in enumerate(zdev):
        cp = rcopy(msg.at[dev[1]], r1.at[h], s1.at[d], q1.at[d], dev)
        cp.start()
        sends.append(cp)
    r1[h] = msg[h]
    for d in range(nz - 1):
        frm = lax.rem(h + nz - 1 - d, nz)
        rcopy(r1.at[frm], r1.at[frm], s1.at[d], q1.at[d], (s, frm)).wait_recv()
    total = jnp.zeros(tot.shape, F32)
    for z in range(nz):
        total = total + wt[z] * r1[z].astype(F32)
    tot[...] = total.astype(BF)
    for d, dev in enumerate(sdev):
        cp = rcopy(tot, r2.at[s], s2.at[d], q2.at[d], dev)
        cp.start()
        sends.append(cp)
    r2[s] = tot[...]
    line = [sum(wl[z, k] * r1[k].astype(F32) for k in range(nz)) for z in range(nz)]
    for d in range(ns - 1):
        frm = jnp.bitwise_xor(s, d + 1)
        rcopy(r2.at[frm], r2.at[frm], s2.at[d], q2.at[d], (frm, h)).wait_recv()
    for k in range(ns):
        got = r2[k].astype(F32)
        line = [line[z] + wp[z, k] * got for z in range(nz)]
    for z in range(nz):
        outb[z] = line[z].astype(BF)
    for d, dev in enumerate(zdev):
        cp = rcopy(outb.at[dev[1]], out.at[h], s3.at[d], q3.at[d], dev)
        cp.start()
        sends.append(cp)
    out[h] = outb[h]
    for d in range(nz - 1):
        frm = lax.rem(h + nz - 1 - d, nz)
        rcopy(out.at[frm], out.at[frm], s3.at[d], q3.at[d], (s, frm)).wait_recv()
    for cp in sends:
        cp.wait_send()


def scan_states(ns, nz, cid, wt, wp, wl, msg):
    dma = pltpu.SemaphoreType.DMA
    one = msg.shape[1:]
    return pl.pallas_call(
        functools.partial(scan_kernel, ns, nz),
        out_shape=jax.ShapeDtypeStruct(msg.shape, BF),
        in_specs=[smem_spec()] * 3 + [vmem_spec()],
        out_specs=vmem_spec(),
        scratch_shapes=[
            pltpu.VMEM(msg.shape, BF),
            pltpu.VMEM((ns,) + one, BF),
            pltpu.VMEM(one, BF),
            pltpu.VMEM(msg.shape, BF),
            dma((nz - 1,)),
            dma((nz - 1,)),
            dma((ns - 1,)),
            dma((ns - 1,)),
            dma((nz - 1,)),
            dma((nz - 1,)),
        ],
        name="scan_states",
        compiler_params=pltpu.CompilerParams(collective_id=cid, has_side_effects=True),
    )(wt, wp, wl, msg)


def add_rows(dst, lead, start, src, src_lead, src_start, n):
    blk = min(n, 32)

    def step(i, _):
        a = dst[lead + (pl.ds(pl.multiple_of(start + i * blk, 16), blk), slice(None))]
        b = src[src_lead + (pl.ds(pl.multiple_of(src_start + i * blk, 16), blk), slice(None))]
        dst[lead + (pl.ds(pl.multiple_of(start + i * blk, 16), blk), slice(None))] = (
            a.astype(F32) + b.astype(F32)
        ).astype(BF)
        return 0

    lax.fori_loop(0, n // blk, step, 0)


def reduce_kernel(ns, nz, lo, gt, gb, *refs):
    s, h = lax.axis_index("seq"), lax.axis_index("head")
    o0, o1 = bit_orders(ns)
    orders = ([0] + o0, [0] + o1)
    m = len(orders[0])
    g = refs[:3]
    lo_out, gt_out, gbo = refs[3:6]
    outs = refs[6:9]
    sc = refs[9:]
    acc = sc[0:3]
    rec = [sc[3 + i * m : 3 + (i + 1) * m] for i in range(3)]
    base = 3 + 3 * m
    zl, zr = sc[base : base + 3], sc[base + 3 : base + 6]
    gcur, grec, gz = sc[base + 6 : base + 9]
    lsem, tsend, trecv, csend, crecv, zsend, zrecv, gsend, grecv = sc[base + 9 :]
    t = lo.shape[0]
    ew = lo_out.shape[1]
    unit = g[0].shape[3] // ns
    zdev = z_others(s, h, nz)
    enter(zdev + [(jnp.bitwise_xor(s, 1 << b), h) for b in orders[0]])
    sends = []
    local = []

    def a2a(i, src, dst):
        for d, dev in enumerate(zdev):
            cp = rcopy(
                src.at[:, pl.ds(dev[1] * ew, ew)],
                dst.at[pl.ds(h * t, t), :],
                tsend.at[i * (nz - 1) + d],
                trecv.at[i * (nz - 1) + d],
                dev,
            )
            cp.start()
            sends.append((None, cp))
        lc = pltpu.make_async_copy(src.at[:, pl.ds(h * ew, ew)], dst.at[pl.ds(h * t, t), :], lsem.at[i])
        lc.start()
        local.append(lc)

    def a2a_wait(i, src, dst):
        for d in range(nz - 1):
            frm = lax.rem(h + nz - 1 - d, nz)
            rcopy(
                src.at[:, pl.ds(h * ew, ew)],
                dst.at[pl.ds(frm * t, t), :],
                tsend.at[i * (nz - 1) + d],
                trecv.at[i * (nz - 1) + d],
                (s, frm),
            ).wait_recv()

    def item(a, tz):
        c = g[a].shape[1]
        idx = a * nz + tz
        pos = [0, 0]
        for j in range(m + 1):
            if j > 0:
                for f in range(2):
                    i = (idx * m + j - 1) * 2 + f
                    n = unit * (ns >> j)
                    buf = rec[a][j - 1].at[tz, :, f]
                    rcopy(buf, buf, csend.at[i], crecv.at[i], (s, h)).wait_recv()
                    if j == 1:
                        pltpu.make_async_copy(
                            acc[a].at[tz, :, f], acc[a].at[tz, :, f], lsem.at[2 + idx * 2 + f]
                        ).wait()
                    for cc in range(c):
                        add_rows(acc[a], (tz, cc, f), pos[f], rec[a][j - 1], (tz, cc, f), 0, n)
            if j < m:
                for f in range(2):
                    i = (idx * m + j) * 2 + f
                    n = unit * (ns >> (j + 1))
                    b = (s >> orders[f][j]) & 1
                    dev = (jnp.bitwise_xor(s, 1 << orders[f][j]), h)
                    if j == 0:
                        src = g[a].at[tz, :, f, pl.ds((1 - b) * n, n), :]
                        lc = pltpu.make_async_copy(
                            g[a].at[tz, :, f, pl.ds(b * n, n), :], acc[a].at[tz, :, f], lsem.at[2 + idx * 2 + f]
                        )
                        lc.start()
                    else:
                        src = acc[a].at[tz, :, f, pl.ds(pl.multiple_of(pos[f] + (1 - b) * n, 16), n), :]
                        pos[f] = pos[f] + b * n
                    cp = rcopy(src, rec[a][j].at[tz, :, f], csend.at[i], crecv.at[i], dev)
                    cp.start()
                    sends.append((None, cp))
            yield
        for d, (buf, cond, first, nb) in enumerate(
            ((zl, h < tz, h >= 1, h + 1), (zr, h > tz, h + 1 < nz, h - 1))
        ):
            for f in range(2):
                i = (idx * 2 + d) * 2 + f
                mine = acc[a].at[tz, :, f, pl.ds(pl.multiple_of(pos[f], 16), unit), :]
                cp = rcopy(mine, buf[a].at[tz, :, f], zsend.at[i], zrecv.at[i], (s, nb))

                def relay(cp=cp, f=f, d=d, buf=buf, first=first):
                    def more():
                        cp.wait_recv()
                        for cc in range(c):
                            add_rows(acc[a], (tz, cc, f), pos[f], buf[a], (tz, cc, f), 0, unit)

                    pl.when(first)(more)
                    cp.start()

                pl.when(cond)(relay)
                sends.append((cond, cp))
        yield

        def finish():
            for f in range(2):
                for d, (buf, there) in enumerate(((zl, tz > 0), (zr, tz < nz - 1))):
                    if there:
                        i = (idx * 2 + d) * 2 + f
                        rcopy(
                            buf[a].at[tz, :, f], buf[a].at[tz, :, f], zsend.at[i], zrecv.at[i], (s, h)
                        ).wait_recv()
                for cc in range(c):
                    v = acc[a][tz, cc, f, pl.ds(pl.multiple_of(pos[f], 16), unit), :].astype(F32)
                    if tz > 0:
                        v = v + zl[a][tz, cc, f].astype(F32)
                    if tz < nz - 1:
                        v = v + zr[a][tz, cc, f].astype(F32)
                    outs[a][cc, f] = v.astype(BF)

        pl.when(h == tz)(finish)

    def small():
        gcur[0] = gb[...]
        for j, b in enumerate(orders[0]):
            dev = (jnp.bitwise_xor(s, 1 << b), h)
            cp = rcopy(gcur.at[j], grec.at[j], gsend.at[j], grecv.at[j], dev)
            cp.start()
            sends.append((None, cp))
            yield
            cp.wait_recv()
            gcur[j + 1] = gcur[j] + grec[j]
        for d, dev in enumerate(zdev):
            cp = rcopy(gcur.at[m], gz.at[h], gsend.at[m + d], grecv.at[m + d], dev)
            cp.start()
            sends.append((None, cp))
        gz[h] = gcur[m]
        yield
        for d in range(nz - 1):
            frm = lax.rem(h + nz - 1 - d, nz)
            rcopy(gz.at[frm], gz.at[frm], gsend.at[m + d], grecv.at[m + d], (s, frm)).wait_recv()
        total = gz[0]
        for z in range(1, nz):
            total = total + gz[z]
        gbo[...] = total

    a2a(0, lo, lo_out)
    order = [2, 1, 0]
    groups = [[item(a, tz)] for a in order for tz in range(nz)]
    groups[1].append(small())
    a2a(1, gt, gt_out)
    run_waves(groups)
    a2a_wait(0, lo, lo_out)
    a2a_wait(1, gt, gt_out)
    for lc in local:
        lc.wait()
    for cond, cp in sends:
        if cond is None:
            cp.wait_send()
        else:
            pl.when(cond)(cp.wait_send)


def reduce_all(ns, nz, lo, gt, gb, g4, gu, gd):
    t, d = lo.shape
    m = ns.bit_length() - 1
    dma = pltpu.SemaphoreType.DMA
    gs = (g4, gu, gd)
    unit = g4.shape[3] // ns

    def bufs(div):
        return [pltpu.VMEM((nz, a.shape[1], 2, a.shape[3] // div, a.shape[4]), BF) for a in gs]

    rec = []
    for i in range(3):
        rec += [bufs(2 << j)[i] for j in range(m)]
    outs = tuple(jax.ShapeDtypeStruct((a.shape[1], 2, unit, a.shape[4]), BF) for a in gs)
    n_items = 3 * nz
    return pl.pallas_call(
        functools.partial(reduce_kernel, ns, nz),
        out_shape=(
            jax.ShapeDtypeStruct((t * nz, d // nz), BF),
            jax.ShapeDtypeStruct((t * nz, d // nz), BF),
            jax.ShapeDtypeStruct(gb.shape, F32),
        )
        + outs,
        in_specs=[any_spec()] * 2 + [vmem_spec()] + [any_spec()] * 3,
        out_specs=(any_spec(),) * 2 + (vmem_spec(),) * 4,
        scratch_shapes=bufs(2)
        + rec
        + bufs(ns)
        + bufs(ns)
        + [
            pltpu.VMEM((m + 1,) + gb.shape, F32),
            pltpu.VMEM((m,) + gb.shape, F32),
            pltpu.VMEM((nz,) + gb.shape, F32),
            dma((2 + 2 * n_items,)),
            dma((2 * (nz - 1),)),
            dma((2 * (nz - 1),)),
            dma((n_items * m * 2,)),
            dma((n_items * m * 2,)),
            dma((n_items * 4,)),
            dma((n_items * 4,)),
            dma((m + nz - 1,)),
            dma((m + nz - 1,)),
        ],
        name="reduce_all",
        compiler_params=pltpu.CompilerParams(
            collective_id=3, has_side_effects=True, vmem_limit_bytes=58 * 2**20
        ),
    )(lo, gt, gb, g4, gu, gd)


def layer_norm(rows, gain, bias):
    mean_row = jnp.mean(rows, axis=-1, keepdims=True)
    centered = rows - mean_row
    variance = jnp.mean(centered * centered, axis=-1, keepdims=True)
    return centered * lax.rsqrt(variance + EPS) * gain + bias


def dot(spec, a, b):
    return jnp.einsum(spec, a, b, preferred_element_type=F32)


def shards(ns, nz, tokens, lengths, pad_mask, w_qkv, w_out, w_up, w_down, norm_gains, norm_biases, out_cotangent):
    rows = tokens.shape[0]
    t = rows // nz
    d = w_qkv.shape[1]
    nh = d // HD
    gh = nh // nz
    ew = d // nz
    blk = math.gcd(t, UNIT)
    nb = t // blk
    s, h = lax.axis_index("seq"), lax.axis_index("head")

    ends = jnp.cumsum(lengths)

    def item_at(p):
        return jnp.sum((p[..., None] >= ends).astype(jnp.int32), axis=-1)

    ndev = ns * nz
    last = item_at((jnp.arange(ndev, dtype=jnp.int32) + 1) * t - 1)
    before = jnp.concatenate([jnp.full((1,), -1, jnp.int32), last[:-1]])
    me = s * nz + h
    chunk = item_at(me * t + jnp.arange(nb, dtype=jnp.int32) * blk)
    prior = lax.dynamic_slice_in_dim(before, me, 1)
    cflag = (chunk == jnp.concatenate([prior, chunk[:-1]])).astype(F32)
    last2, before2 = last.reshape(ns, nz), before.reshape(ns, nz)
    my_last, my_before = last2[s], before2[s]
    sidx, zidx = jnp.arange(ns), jnp.arange(nz)
    fwt = (my_last == my_last[-1]).astype(F32)
    fwp = ((sidx[None, :] < s) & (last2[None, :, -1] == my_before[:, None])).astype(F32)
    fwl = ((zidx[None, :] < zidx[:, None]) & (my_last[None, :] == my_before[:, None])).astype(F32)
    bwt = (my_before == my_before[0]).astype(F32)
    bwp = ((sidx[None, :] > s) & (before2[None, :, 0] == my_last[:, None])).astype(F32)
    bwl = ((zidx[None, :] > zidx[:, None]) & (my_before[None, :] == my_last[:, None])).astype(F32)

    w4 = jnp.concatenate([w_qkv, w_out.T[None]], axis=0)
    x, co, w4g, wug, wdg = gather_all(ns, nz, tokens, out_cotangent, w4, w_up[None], w_down[None])
    wug, wdg = wug[:, 0], wdg[:, 0]
    pad = lax.dynamic_slice_in_dim(pad_mask, h * t, t).astype(F32)[:, None]
    xf = x.astype(F32)
    a1f, pull1 = jax.vjp(layer_norm, xf, norm_gains[0], norm_biases[0])
    a1 = a1f.astype(BF)
    qkv = dot("td,hcde->cthe", a1, w4g[:, :3]).reshape(3, t, d)
    q, k = qkv[0], qkv[1]
    fq = jnp.where(q > 0, q + 1.0, jnp.exp(jnp.minimum(q, 0.0))).astype(BF)
    fk = (pad * jnp.where(k > 0, k + 1.0, jnp.exp(jnp.minimum(k, 0.0)))).astype(BF)
    vb = qkv[2].astype(BF)

    def heads(a):
        return a.reshape(nb, blk, nh, HD)

    fqh, fkh, vbh = heads(fq), heads(fk), heads(vb)
    inc = dot("nuhk,nuhv->nhkv", fkh, vbh)
    zinc = jnp.sum(fkh.astype(F32), axis=1)

    def pack(state, norm):
        m1 = state.reshape(nz, gh, HD, HD).transpose(0, 2, 1, 3).reshape(nz, HD, ew)
        m2 = jnp.pad(norm.reshape(nz, 1, ew), ((0, 0), (0, MSG - HD - 1), (0, 0)))
        return jnp.concatenate([m1, m2], axis=1).astype(BF)

    def unpack(msg):
        msg = msg.astype(F32)
        st = msg[:, :HD].reshape(nz, HD, gh, HD).transpose(0, 2, 1, 3).reshape(nh, HD, HD)
        return st, msg[:, HD].reshape(nh, HD)

    sl, zl = inc[0], zinc[0]
    for n in range(1, nb):
        sl, zl = cflag[n] * sl + inc[n], cflag[n] * zl + zinc[n]
    st, zt = unpack(scan_states(ns, nz, 1, fwt, fwp, fwl, pack(sl, zl)))
    states, norms = [], []
    for n in range(nb):
        states.append(cflag[n] * st)
        norms.append(cflag[n] * zt)
        st, zt = cflag[n] * st + inc[n], cflag[n] * zt + zinc[n]
    states = jnp.stack(states).astype(BF)
    norms = jnp.stack(norms)
    causal = (jnp.arange(blk)[:, None] >= jnp.arange(blk)[None, :]).astype(F32)
    scores = (causal * dot("nthk,nuhk->nhtu", fqh, fkh)).astype(BF)
    numer = dot("nhtu,nuhv->nthv", scores, vbh) + dot("nthk,nhkv->nthv", fqh, states)
    ks = dot("tu,nuhk->nthk", causal.astype(BF), fkh) + norms[:, None]
    den = 1.0 + jnp.sum(fqh.astype(F32) * ks, axis=-1)
    att = (numer / den[..., None]).reshape(t, d).astype(BF)
    wot = w4g[:, 3]
    mid = xf + dot("the,hde->td", att.reshape(t, nz, ew), wot)
    a2f, pull2 = jax.vjp(layer_norm, mid, norm_gains[1], norm_biases[1])
    a2 = a2f.astype(BF)
    up = dot("td,hdf->thf", a2, wug)
    gel, pullg = jax.vjp(jax.nn.gelu, up)
    hid = gel.astype(BF)
    lo = (mid + dot("thf,hfd->td", hid, wdg)).astype(BF)
    d_up = pullg(dot("td,hfd->thf", co, wdg))[0].astype(BF)
    d_a2 = dot("thf,hdf->td", d_up, wug)
    d_mid_n, gain2, bias2 = pull2(d_a2)
    d_mid = co.astype(F32) + d_mid_n
    dml = d_mid.astype(BF)
    d_att = dot("td,hde->the", dml, wot).reshape(nb, blk, nh, HD)
    d_num = (d_att / den[..., None]).astype(BF)
    d_den = -jnp.sum(d_att * numer, axis=-1) / (den * den)
    d_ks = d_den[..., None] * fqh.astype(F32)
    gloc = dot("nthk,nthv->nhkv", fqh, d_num)
    yloc = jnp.sum(d_ks, axis=1)
    sl, zl = cflag[nb - 1] * gloc[nb - 1], cflag[nb - 1] * yloc[nb - 1]
    for n in range(nb - 2, -1, -1):
        sl, zl = cflag[n] * (sl + gloc[n]), cflag[n] * (zl + yloc[n])
    st, zt = unpack(scan_states(ns, nz, 2, bwt, bwp, bwl, pack(sl, zl)))
    d_inc, d_zinc = [None] * nb, [None] * nb
    for n in range(nb - 1, -1, -1):
        d_inc[n], d_zinc[n] = st, zt
        st, zt = cflag[n] * (st + gloc[n]), cflag[n] * (zt + yloc[n])
    d_inc = jnp.stack(d_inc).astype(BF)
    d_zinc = jnp.stack(d_zinc)
    d_scores = (causal * dot("nthv,nuhv->nhtu", d_num, vbh)).astype(BF)
    d_fq = (
        d_den[..., None] * ks
        + dot("nthv,nhkv->nthk", d_num, states)
        + dot("nhtu,nuhk->nthk", d_scores, fkh)
    )
    d_fk = (
        dot("tu,nthk->nuhk", causal.astype(BF), d_ks.astype(BF))
        + dot("nhtu,nthk->nuhk", d_scores, fqh)
        + dot("nuhv,nhkv->nuhk", vbh, d_inc)
        + d_zinc[:, None]
    )
    d_v = dot("nhtu,nthv->nuhv", scores, d_num) + dot("nuhk,nhkv->nuhv", fkh, d_inc)
    d_q = (d_fq.reshape(t, d) * jnp.where(q > 0, 1.0, jnp.exp(jnp.minimum(q, 0.0)))).astype(BF)
    d_k = (d_fk.reshape(t, d) * pad * jnp.where(k > 0, 1.0, jnp.exp(jnp.minimum(k, 0.0)))).astype(BF)
    d_qkv = jnp.stack([d_q, d_k, d_v.reshape(t, d).astype(BF)]).reshape(3, t, nz, ew)
    d_a1 = dot("cthe,hcde->td", d_qkv, w4g[:, :3])
    d_x, gain1, bias1 = pull1(d_a1)
    gt = (d_mid + d_x).astype(BF)

    o0, o1 = bit_orders(ns)
    m = ns.bit_length() - 1

    def perm(a):
        u = d // (2 * ns)
        a = a.reshape((t,) + (2,) * m + (2, u))
        parts = []
        for f, order in enumerate(([0] + o0, [0] + o1)):
            v = a[..., f, :]
            v = v.transpose((0,) + tuple(m - b for b in order) + (m + 1,))
            parts.append(v.reshape(t, d // 2))
        return jnp.concatenate(parts, axis=1)

    a1p = perm(a1)
    g_qkv = dot("td,cthe->hcde", a1p, d_qkv).astype(BF)
    g_out = dot("td,the->hde", perm(dml), att.reshape(t, nz, ew)).astype(BF)
    g4 = jnp.concatenate([g_qkv, g_out[:, None]], axis=1).reshape(nz, 4, 2, d // 2, ew)
    ff = w_up.shape[1]
    gu = dot("td,thf->hdf", perm(a2), d_up).astype(BF).reshape(nz, 1, 2, d // 2, ff)
    gd = dot("td,thf->hdf", perm(co), hid).astype(BF).reshape(nz, 1, 2, d // 2, ff)
    gb = jnp.concatenate([jnp.stack([gain1, gain2, bias1, bias2]), jnp.zeros((4, d), F32)])
    lo_o, gt_o, gbo, o4, ou, od = reduce_all(ns, nz, lo, gt, gb, g4, gu, gd)
    piece = d // ns
    o4 = o4.reshape(4, piece, ew).astype(F32)
    w = d // ndev
    gbs = lax.dynamic_slice_in_dim(gbo, (h * ns + s) * w, w, 1)
    return (
        lo_o,
        gt_o.astype(F32),
        o4[:3],
        o4[3].T,
        ou.reshape(piece, ff).astype(F32),
        od.reshape(piece, ff).astype(F32).T,
        gbs[:2],
        gbs[2:4],
    )


def solution(mesh):
    in_specs = (
        P("seq", "head"),
        P(),
        P("seq"),
        P(None, None, "head"),
        P("head", None),
        P(None, "head"),
        P("head", None),
        P(),
        P(),
        P("seq", "head"),
    )
    out_specs = (
        P("seq", "head"),
        P("seq", "head"),
        P(None, "seq", "head"),
        P("head", "seq"),
        P("seq", "head"),
        P("head", "seq"),
        P(None, ("head", "seq")),
        P(None, ("head", "seq")),
    )
    f = functools.partial(shards, mesh.shape["seq"], mesh.shape["head"])
    return jax.shard_map(f, mesh=mesh, in_specs=in_specs, out_specs=out_specs, check_vma=False)
```

time: 1480 us -> 779 us (0.53)
  waiting for transfers between devices: 1030 us -> 0 us
  Pallas kernels: 0 us -> 427 us
  blocking collectives: 54.3 us -> 0 us
  other arithmetic: 94.6 us -> 61.2 us
  local copies, waits for them, and re-layouts: 120 us -> 137 us
    pallas_call x0 -> x4, Pallas kernels: none -> 427 us  [the longest x1 214 us: gather_all(): pl.pallas_call(functools.partial(gather_kernel, ns, nz), out_shape=(jax.S...]
    all_gather x4 -> x0, waiting for transfers between devices: 360 us -> none  [the longest x1 156 us: shards(): middle_full = lax.all_gather(middle, 'head', axis=1, tiled=True)]
    psum x2 -> x0, waiting for transfers between devices: 341 us -> none  [norm_back(): lax.psum(partial_grad.astype(jnp.bfloat16), 'head').astype(jnp.float32)]
    reduce_scatter x3 -> x0, waiting for transfers between devices: 185 us -> none  [the longest x1 160 us: shards(): lax.psum_scatter(attn_terms, 'head', scatter_dimension=1, tiled=True)]
    unnamed x19 -> x0, waiting for transfers between devices: 142 us -> none
    all_gather x4 -> x0, blocking collectives: 40.2 us -> none  [entering(): lax.all_gather(part.astype(kind), axis)]
    convert_element_type x4 -> x13, local copies, waits for them, and re-layouts: 10.6 us -> 47.2 us  [the longest x3 10.2 us: shards(): d_v.reshape(t, d).astype(BF)]
    unnamed x132 -> x146, local copies, waits for them, and re-layouts: 36.6 us -> 12.2 us
  transfers between devices with their start and end apart: 14 -> 0, of which waited for: 12 -> 0; matrix products, arithmetic and copies ran while one was open for 13% -> 0% of each run, Pallas kernels for 0% -> 0%
where the time goes in v1:
time: 779 us; the launch traced here: 773 us
  Pallas kernels  427 us (55%)
  matrix products  145 us (19%)
  local copies, waits for them, and re-layouts  137 us (18%)
  other arithmetic  61.2 us (8%)
    pallas_call x1, Pallas kernels, gather_all(): pl.pallas_call(functools.partial(gather_kernel, ns, nz), out_shape=(jax.S...  214 us
    pallas_call x1, Pallas kernels, reduce_all(): pl.pallas_call(functools.partial(reduce_kernel, ns, nz), out_shape=(jax.S...  173 us
    dot_general x26, matrix products, dot(): return jnp.einsum(spec, a, b, preferred_element_type=F32)  145 us
    pallas_call x2, Pallas kernels, scan_states(): pl.pallas_call(functools.partial(scan_kernel, ns, nz), out_shape=jax.Shap...  39.9 us

profile of v1, /device:TPU:24, one launch (start us, length us, event | category | flops | bytes accessed | tf_op | source)
XLA Modules:
  0.0 772.7 jit_solution(5793873031660710729)
XLA Ops:
  1.9 2.9 pad_maximum_fusion.2.w4
  4.8 214.0 %gather_all.1 = (bf16[576,1024]{1,0:T(8,128)(2,1)}, bf16[576,1024]{1,0:T(8,128)(2,1)}, bf16[4,4,1024,256]{3,2,1,0:T(8,128)(2,1)}, bf16[4,1,1024,1024]{3,2,1,0:T(8,128)(2,1)}, bf16[4,1,1024,1024]{3,2,1,0:T(8,128)(2,1)}) custom-call(bf16[2304,256]{1,0:T(8,128)(2,1)} %tok.1, bf16[2304,256]{1,0:T(8,128)(2,1)} %cot.1, ...), custom_call_target="tpu_custom_call" | custom-call | tf_op jit(solution)/shard_map/gather_all/pallas_call | solution.py:193
  223.3 6.4 convolution_bitcast_fusion
  229.7 4.0 select_convert_fusion
  233.9 3.2 copy.325
  237.2 6.0 select_n.48
  244.0 2.8 convert_reduce_fusion.1
  254.6 2.8 slice.344
  257.4 2.4 copy.323
  259.8 5.3 convert_element_type.217
  265.1 2.2 fusion.72
  270.9 20.0 %scan_states.2 = bf16[4,80,256]{2,1,0:T(8,128)(2,1)} custom-call(f32[4]{0:T(128)} %compare_convert_fusion.1.wt, f32[4,8]{1,0:T(4,128)} %and_convert_fusion.1.wp, f32[4,4]{1,0:T(4,128)} %get-tuple-element.78.wl, bf16[4,80,256]{2,1,0:T(8,128)(2,1)} %fusion.79.msg), custom_call_target="tpu_custom_call" | custom-call | tf_op jit(solution)/shard_map/scan_states/pallas_call | solution.py:265
  295.4 4.8 convert_element_type.220
  300.2 4.1 fusion.25
  311.5 2.5 fusion.26
  314.1 2.7 copy.340
  316.8 5.2 convert_element_type.235
  321.9 3.6 fusion.121
  327.7 11.1 %fusion.13 = f32[576,4,1024]{2,0,1:T(8,128)} fusion(bf16[4,1,1024,1024]{3,2,1,0:T(8,128)(2,1)} %get-tuple-element.21, bf16[576,1024]{1,0:T(8,128)(2,1)S(1)} %add_convert_fusion.2), kind=kOutput, calls=%fused_computation.19 | convolution fusion | flops 4831838208 | bytes 19005440 | tf_op jit(solution)/shard_map/td,hdf->thf/dot_general | solution.py:524
  338.8 9.9 %fusion.39.lo = bf16[576,1024]{1,0:T(8,128)(2,1)} fusion(f32[576,1024]{1,0:T(8,128)S(1)} %get-tuple-element.87, bf16[4,1,1024,1024]{3,2,1,0:T(8,128)(2,1)S(1)} %bitcast.333, f32[576,4,1024]{2,0,1:T(8,128)} %fusion.13), kind=kOutput, calls=%fused_computation.72 | convolution fusion | flops 4854251520 | bytes 21364736 | tf_op jit(solution)/shard_map/thf,hfd->td/dot_general | solution.py:524
  348.7 18.2 %fusion.6 = bf16[576,4,1024]{2,0,1:T(8,128)(2,1)} fusion(f32[576,4,1024]{2,0,1:T(8,128)} %fusion.13, bf16[4,1,1024,1024]{3,2,1,0:T(8,128)(2,1)} %get-tuple-element.22, bf16[576,1024]{1,0:T(8,128)(2,1)S(1)} %copy-done.19), kind=kOutput, calls=%fused_computation.8 | convolution fusion | flops 4879024128 | bytes 23724032 | tf_op jit(solution)/shard_map/td,hfd->thf/dot_general | solution.py:524
  366.9 8.6 %fusion.38 = (f32[1024]{0:T(1024)}, f32[576]{0:T(1024)S(1)}, f32[1024]{0:T(1024)}, f32[576,1024,1]{1,0,2:T(8,128)S(1)}) fusion(f32[576,1024]{1,0:T(8,128)S(1)} %get-tuple-element.87, f32[576]{0:T(1024)S(1)} %fusion.92, f32[576]{0:T(1024)S(1)} %broadcast_multiply_fusion, f32[1024]{0:T(1024)S(1)} %bitcast.314, bf16[576,4,1024]{2,0,1:T(8,128)(2,1)} %fusion.6, ...), kind=kOutput, calls=%fused_computation.70 | convolution fusion | flops 4836554240 | bytes 17844992 | tf_op jit(solution)/shard_map/thf,hdf->td/dot_general | solution.py:524
  378.1 3.1 slice_bitcast_fusion
  381.2 4.2 copy.342
  385.4 4.8 fusion.27
  390.2 5.6 fusion.122
  398.2 2.4 fusion.88
  402.0 2.0 fusion.108
  405.1 2.0 fusion.64
  411.5 19.9 %scan_states.3 = bf16[4,80,256]{2,1,0:T(8,128)(2,1)} custom-call(f32[4]{0:T(128)} %compare_convert_fusion.wt, f32[4,8]{1,0:T(4,128)} %and_convert_fusion.wp, f32[4,4]{1,0:T(4,128)} %get-tuple-element.77.wl, bf16[4,80,256]{2,1,0:T(8,128)(2,1)} %fusion.80.msg), custom_call_target="tpu_custom_call" | custom-call | tf_op jit(solution)/shard_map/scan_states/pallas_call | solution.py:265
  433.0 2.0 reshape.481
  436.2 2.6 multiply_convert_fusion.5
  438.8 2.7 fusion.50
  441.6 2.7 copy.355
  444.3 5.1 convert_element_type.253
  449.4 2.4 copy.356
  451.9 2.4 fusion.69
  457.0 2.3 bitcast_add_fusion
  459.3 4.2 copy.344
  463.5 6.0 reshape.479
  469.6 3.1 copy.345
  472.7 2.3 fusion.45
  476.2 2.6 fusion.110
  480.8 4.4 add_bitcast_fusion
  485.2 4.2 copy.352
  489.4 6.0 reshape.483
  495.5 3.4 copy.353
  498.9 5.1 multiply_convert_fusion.4
  504.1 7.6 bitcast_reduce_fusion
  513.7 2.0 add_convert_fusion.1.gt
  518.8 4.4 convert_bitcast_fusion.1
  523.3 2.8 copy.372
  526.1 2.4 copy.359
  528.5 2.3 slice_bitcast_fusion.8
  531.7 2.2 copy.363
  533.8 2.0 copy.360
  535.8 2.1 copy.362
  538.0 8.8 %convert_bitcast_fusion = bf16[4,3,1024,256]{2,3,0,1:T(8,128)(2,1)} fusion(bf16[576,512]{1,0:T(8,128)(2,1)} %copy.363, bf16[576,512]{1,0:T(8,128)(2,1)} %copy.362, bf16[1,576,4,256]{3,1,0,2:T(8,128)(2,1)} %copy.356, bf16[1,576,4,256]{3,1,0,2:T(8,128)(2,1)} %copy-done.33, bf16[1,576,4,256]{3,1,0,2:T(8,128)(2,1)} %copy-done.32), kind=kOutput, calls=%fused_computation.25 | convolution fusion | flops 3632922624 | bytes 11010048 | tf_op jit(solution)/shard_map/td,cthe->hcde/dot_general | solution.py:524
  546.7 8.7 %copy.365 = bf16[4,3,1024,256]{3,2,1,0:T(8,128)(2,1)} copy(bf16[4,3,1024,256]{2,3,0,1:T(8,128)(2,1)} %convert_bitcast_fusion) | data formatting | bytes 12582912 | tf_op jit(solution)/shard_map/convert_element_type | solution.py:670
  555.5 6.8 pad_maximum_fusion.refs_0_
  564.9 12.2 %convolution_convert_fusion.1 = bf16[4,1024,1024]{1,2,0:T(8,128)(2,1)} fusion(bf16[576,4,1024]{2,0,1:T(8,128)(2,1)} %fusion.6, bf16[576,512]{1,0:T(8,128)(2,1)S(1)} %copy.377, bf16[576,512]{1,0:T(8,128)(2,1)S(1)} %copy.376), kind=kOutput, calls=%fused_computation.22 | convolution fusion | flops 4838391808 | bytes 14286848 | tf_op jit(solution)/shard_map/td,thf->hdf/dot_general | solution.py:524
  578.6 11.7 %convolution_convert_fusion = bf16[4,1024,1024]{1,2,0:T(8,128)(2,1)} fusion(bf16[576,512]{1,0:T(8,128)(2,1)S(1)} %copy.382, bf16[576,512]{1,0:T(8,128)(2,1)S(1)} %copy.381, f32[576,4,1024]{2,0,1:T(8,128)} %fusion.13), kind=kOutput, calls=%fused_computation.21 | convolution fusion | flops 4859625472 | bytes 19005440 | tf_op jit(solution)/shard_map/td,thf->hdf/dot_general | solution.py:524
  590.2 173.4 %reduce_all.1 = (bf16[2304,256]{1,0:T(8,128)(2,1)}, bf16[2304,256]{1,0:T(8,128)(2,1)}, f32[8,1024]{1,0:T(8,128)}, bf16[4,2,64,256]{3,2,1,0:T(8,128)(2,1)}, bf16[...) custom-call(bf16[576,1024]{1,0:T(8,128)(2,1)} %fusion.39.lo, bf16[576,1024]{1,0:T(8,128)(2,1)} %add_convert_fusion.1.gt, ...), custom_call_target="tpu_custom_call" | custom-call | tf_op jit(solution)/shard_map/reduce_all/pallas_call | solution.py:481
  763.7 2.9 convert_element_type.263
  (255 shorter events, 68.3 us)
Async XLA Ops:
  4.8 214.0 %copy-start.58 = (f32[2,1024]{1,0:T(2,128)S(1)}, f32[2,1024]{1,0:T(2,128)}, u32[]{:S(2)}) copy-start(f32[2,1024]{1,0:T(2,128)} %param.18) | copy-start | bytes 24580
  4.8 214.6 %copy-start.59 = (f32[2,1024]{1,0:T(2,128)S(1)}, f32[2,1024]{1,0:T(2,128)}, u32[]{:S(2)}) copy-start(f32[2,1024]{1,0:T(2,128)} %param.17) | copy-start | bytes 24580
  218.8 3.9 copy-start.11
  219.4 3.8 copy-start.49
  220.9 2.3 copy-start.45
  222.7 7.0 copy-start.53
  223.3 6.4 copy-start.23
  229.7 4.3 copy-start.14
  244.0 2.9 copy-start.66
  246.8 18.3 %copy-start.1 = (bf16[3,192,16,64]{1,3,2,0:T(8,128)(2,1)}, bf16[3,192,16,64]{1,3,2,0:T(8,128)(2,1)S(1)}, u32[]{:S(2)}) copy-start(bf16[3,192,16,64]{1,3,2,0:T(8,128)(2,1)S(1)} %get-tuple-element.44) | copy-start | bytes 3538948
  249.5 10.3 %copy-start.55 = (s32[8,4]{1,0:T(8,128)}, s32[8,4]{1,0:T(8,128)S(1)}, u32[]{:S(2)}) copy-start(s32[8,4]{1,0:T(8,128)S(1)} %reshape.477) | copy-start | bytes 388
  249.5 10.3 %copy-start.60 = (s32[1,4]{1,0:T(1,128)}, s32[1,4]{1,0:T(1,128)S(1)}, u32[]{:S(2)}) copy-start(s32[1,4]{1,0:T(1,128)S(1)} %get-tuple-element.93) | copy-start | bytes 52
  249.5 10.3 %copy-start.62 = (s32[1,4]{1,0:T(1,128)}, s32[1,4]{1,0:T(1,128)S(1)}, u32[]{:S(2)}) copy-start(s32[1,4]{1,0:T(1,128)S(1)} %get-tuple-element.92) | copy-start | bytes 52
  268.4 25.5 %copy-start.21 = (bf16[1,576,4,256]{3,1,0,2:T(8,128)(2,1)S(1)}, bf16[1,576,4,256]{3,1,0,2:T(8,128)(2,1)}, u32[]{:S(2)}) copy-start(bf16[1,576,4,256]{3,1,0,2:T(8,128)(2,1)} %get-tuple-element.45) | copy-start | bytes 3538948
  300.2 4.8 copy-start.2
  305.0 6.6 copy-start.51
  305.0 1.6 copy-start.7
  306.6 2.1 copy-start
  306.6 2.1 copy-start.24
  311.4 2.6 copy-start.37
  311.4 2.6 copy-start.38
  311.5 2.6 copy-start.36
  326.2 12.5 %slice-start.2 = ((s8[8388608]{0:T(1024)(128)(4,1)}), s8[4194304]{0:T(1024)(128)(4,1)S(1)}, s32[]{:S(2)}) async-start(s8[8388608]{0:T(1024)(128)(4,1)} %bitcast.332), calls=%async_computation.2 | async-start | bytes 8388608
  327.7 11.1 %slice-start.3 = ((s8[8388608]{0:T(1024)(128)(4,1)}), s8[4194304]{0:T(1024)(128)(4,1)S(1)}, s32[]{:S(2)}) async-start(s8[8388608]{0:T(1024)(128)(4,1)} %bitcast.332), calls=%async_computation.3 | async-start | bytes 8388608
  338.8 9.9 %copy-start.19 = (bf16[576,1024]{1,0:T(8,128)(2,1)S(1)}, bf16[576,1024]{1,0:T(8,128)(2,1)}, u32[]{:S(2)}) copy-start(bf16[576,1024]{1,0:T(8,128)(2,1)} %get-tuple-element.23) | copy-start | bytes 3538948
  338.8 28.1 %slice-start = ((s8[8388608]{0:T(1024)(128)(4,1)}), s8[4194304]{0:T(1024)(128)(4,1)S(1)}, s32[]{:S(2)}) async-start(s8[8388608]{0:T(1024)(128)(4,1)} %bitcast.330), calls=%async_computation | async-start | bytes 8388608
  348.7 18.2 %slice-start.1 = ((s8[8388608]{0:T(1024)(128)(4,1)}), s8[4194304]{0:T(1024)(128)(4,1)S(1)}, s32[]{:S(2)}) async-start(s8[8388608]{0:T(1024)(128)(4,1)} %bitcast.330), calls=%async_computation.1 | async-start | bytes 8388608
  376.3 1.8 copy-start.12
  381.2 4.2 copy-start.52
  390.1 5.6 copy-start.9
  390.2 5.6 copy-start.63
  390.2 6.1 copy-start.56
  390.2 6.2 copy-start.61
  390.2 6.2 copy-start.67
  390.2 6.9 copy-start.41
  435.0 3.9 copy-start.3
  436.2 5.4 copy-start.25
  438.8 2.8 copy-start.27
  438.8 2.8 copy-start.28
  451.8 2.4 copy-start.8
  451.9 2.7 copy-start.10
  454.6 1.5 copy-start.4
  454.6 2.4 copy-start.15
  457.0 2.3 copy-start.5
  472.7 3.5 copy-start.6
  476.2 2.6 copy-start.31
  476.2 4.7 copy-start.26
  495.5 3.4 copy-start.29
  495.5 3.4 copy-start.30
  498.9 5.2 copy-start.34
  498.9 5.2 copy-start.46
  498.9 5.2 copy-start.50
  504.0 7.7 copy-start.32
  504.0 7.7 copy-start.33
  504.1 7.7 copy-start.54
  504.1 7.7 copy-start.48
  511.7 1.7 copy-start.13
  511.7 2.0 copy-start.20
  513.7 2.0 copy-start.64
  513.7 2.0 copy-start.65
  763.6 3.0 copy-start.39
  763.6 4.5 copy-start.43
  763.7 5.4 copy-start.42
  766.6 4.8 copy-start.35
  (8 other events, 7.2 us)

commit v2 on v1

--- a/solution.py
+++ b/solution.py
@@ -14,7 +14,6 @@
 MESH = pl.DeviceIdType.MESH
 BF = jnp.bfloat16
 F32 = jnp.float32
-MSG = 80
 
 
 def bit_orders(ns):
@@ -513,24 +512,896 @@
     )(lo, gt, gb, g4, gu, gd)
 
 
-def layer_norm(rows, gain, bias):
-    mean_row = jnp.mean(rows, axis=-1, keepdims=True)
-    centered = rows - mean_row
-    variance = jnp.mean(centered * centered, axis=-1, keepdims=True)
-    return centered * lax.rsqrt(variance + EPS) * gain + bias
-
-
-def dot(spec, a, b):
-    return jnp.einsum(spec, a, b, preferred_element_type=F32)
+def dot(a, b):
+    return lax.dot_general(a, b, (((1,), (0,)), ((), ())), preferred_element_type=F32)
+
+
+def dot_t(a, b):
+    return lax.dot_general(a, b, (((1,), (1,)), ((), ())), preferred_element_type=F32)
+
+
+def t_dot(a, b):
+    return lax.dot_general(a, b, (((0,), (0,)), ((), ())), preferred_element_type=F32)
+
+
+def lane_low(shape):
+    return lax.broadcasted_iota(jnp.int32, shape, 1) < HD
+
+
+def row_low(shape):
+    return lax.broadcasted_iota(jnp.int32, shape, 0) < HD
+
+
+def row_block(t):
+    return 96 if t % 96 == 0 else 32
+
+
+def over_rows(t, body):
+    rb = row_block(t)
+
+    def step(i, _):
+        body(pl.ds(pl.multiple_of(i * rb, 32), rb))
+        return 0
+
+    lax.fori_loop(0, t // rb, step, 0)
+
+
+def normed(v):
+    mean = jnp.mean(v, axis=1, keepdims=True)
+    c = v - mean
+    w = lax.rsqrt(jnp.mean(c * c, axis=1, keepdims=True) + EPS)
+    return c * w, w
+
+
+def norm_forward(src, gain, bias, dst):
+    def body(rows):
+        xh, _ = normed(src[rows, :].astype(F32))
+        dst[rows, :] = (xh * gain[...] + bias[...]).astype(BF)
+
+    over_rows(src.shape[0], body)
+
+
+def norm_backward(e_ref, src, gain, add, emit, sums):
+    sums[0] = jnp.zeros(sums.shape[1:], F32)
+    sums[1] = jnp.zeros(sums.shape[1:], F32)
+
+    def body(rows):
+        e = e_ref[rows, :]
+        xh, w = normed(src[rows, :].astype(F32))
+        eg = e * gain[...]
+        m1 = jnp.mean(eg, axis=1, keepdims=True)
+        m2 = jnp.mean(eg * xh, axis=1, keepdims=True)
+        emit(rows, add[rows, :].astype(F32) + w * (eg - m1 - xh * m2))
+        n = e.shape[0]
+        sums[0] += jnp.sum((e * xh).reshape(n // 8, 8, -1), axis=0)
+        sums[1] += jnp.sum(e.reshape(n // 8, 8, -1), axis=0)
+
+    over_rows(src.shape[0], body)
+
+
+def transpose_perm(ns, src, dst):
+    d = dst.shape[0]
+    u = d // (2 * ns)
+    o0, o1 = bit_orders(ns)
+    m = ns.bit_length() - 1
+    orders = ([0] + o0, [0] + o1)
+    for j in range(d // 128):
+        tr = src[:, j * 128 : (j + 1) * 128].T
+        for i in range(128 // u):
+            g = j * (128 // u) + i
+            dev, f = g // 2, g % 2
+            q = sum(((dev >> b) & 1) << (m - 1 - k) for k, b in enumerate(orders[f]))
+            row = f * (d // 2) + q * u
+            dst[row : row + u, :] = tr[i * u : (i + 1) * u, :]
+
+
+def phi(y):
+    return jnp.where(y > 0, y + 1.0, jnp.exp(jnp.minimum(y, 0.0)))
+
+
+def cols(i, n):
+    return pl.ds(pl.multiple_of(i * n, 128), n)
+
+
+def project(a1, wg, g, pad, fq, fk, vb):
+    ew = wg.shape[3]
+    c = cols(g, ew)
+    fq[:, c] = phi(dot(a1[...], wg[g, 0])).astype(BF)
+    fk[:, c] = (pad[...] * phi(dot(a1[...], wg[g, 1]))).astype(BF)
+    vb[:, c] = dot(a1[...], wg[g, 2]).astype(BF)
+
+
+def with_ones(v2):
+    one = jnp.ones_like(v2)
+    low = lane_low(v2.shape)
+    return jnp.where(low, v2, one), jnp.where(low, one, v2)
+
+
+def chunk_sums(p, blk, nb, fk, vb, inc):
+    for n in range(nb):
+        rows = pl.ds(n * blk, blk)
+        k2, v2 = fk[rows, cols(p, 128)], vb[rows, cols(p, 128)]
+        r = t_dot(k2, jnp.concatenate(with_ones(v2), axis=1))
+        inc[n, p] = jnp.where(row_low((128, 128)), r[:, :128], r[:, 128:])
+
+
+def causal_mask(blk):
+    return lax.broadcasted_iota(jnp.int32, (blk, blk), 0) >= lax.broadcasted_iota(jnp.int32, (blk, blk), 1)
+
+
+def masked_scores(a2, b2, keep):
+    low = lane_low(b2.shape)
+    zero = jnp.zeros_like(b2)
+    return [
+        jnp.where(keep, dot_t(a2, b), 0.0).astype(BF)
+        for b in (jnp.where(low, b2, zero), jnp.where(low, zero, b2))
+    ]
+
+
+def split_state(st):
+    low = row_low(st.shape)
+    zero = jnp.zeros_like(st)
+    return jnp.concatenate([jnp.where(low, st, zero), jnp.where(low, zero, st)], axis=1)
+
+
+def attend(p, n, blk, fq, fk, vb, st):
+    rows = pl.ds(n * blk, blk)
+    c = cols(p, 128)
+    q2, k2, v2 = fq[rows, c], fk[rows, c], vb[rows, c]
+    s0, s1 = masked_scores(q2, k2, causal_mask(blk))
+    g0, g1 = with_ones(v2)
+    r = dot(q2, split_state(st))
+    return dot(s0, g0) + r[:, :128], dot(s1, g1) + r[:, 128:]
+
+
+def attend_store(p, n, blk, r0, r1, att, rden):
+    rows = pl.ds(n * blk, blk)
+    low = lane_low(r0.shape)
+    num = jnp.where(low, r0, r1)
+    den = 1.0 + pltpu.roll(jnp.where(low, r1, r0), HD, 1)
+    rd = 1.0 / den
+    att[rows, cols(p, 128)] = (num * rd).astype(BF)
+    rden[rows, cols(p, 128)] = rd
+
+
+def attend_gradient(p, n, blk, datt, att, rden, dr0, dr1):
+    rows = pl.ds(n * blk, blk)
+    c = cols(p, 128)
+    e = datt[rows, c]
+    rd = rden[rows, c]
+    low = lane_low(e.shape)
+    lane = lax.broadcasted_iota(jnp.int32, e.shape, 1)
+    dn = e * rd
+    w = dn * att[rows, c].astype(F32)
+    d0 = -jnp.sum(jnp.where(low, w, 0.0), axis=1, keepdims=True)
+    d1 = -jnp.sum(jnp.where(low, 0.0, w), axis=1, keepdims=True)
+
+    def parts(dd, first):
+        hi = dd.astype(BF).astype(F32)
+        return jnp.where(lane == first, hi, jnp.where(lane == first + 1, dd - hi, 0.0))
+
+    dr0[rows, c] = jnp.where(low, dn, parts(d0, HD)).astype(BF)
+    dr1[rows, c] = jnp.where(low, parts(d1, 0), dn).astype(BF)
+
+
+def chunk_gradients(p, blk, nb, fq, dr0, dr1, ginc):
+    for n in range(nb):
+        rows = pl.ds(n * blk, blk)
+        c = cols(p, 128)
+        r = t_dot(fq[rows, c], jnp.concatenate([dr0[rows, c], dr1[rows, c]], axis=1))
+        ginc[n, p] = jnp.where(row_low((128, 128)), r[:, :128], r[:, 128:])
+
+
+def attend_backward(p, n, blk, fq, fk, vb, dr0, dr1, st, dst, dq, dk, dv):
+    rows = pl.ds(n * blk, blk)
+    c = cols(p, 128)
+    q2, k2, v2, e0, e1 = fq[rows, c], fk[rows, c], vb[rows, c], dr0[rows, c], dr1[rows, c]
+    g0, g1 = with_ones(v2)
+    keep = causal_mask(blk)
+    keep_t = lax.broadcasted_iota(jnp.int32, (blk, blk), 0) <= lax.broadcasted_iota(jnp.int32, (blk, blk), 1)
+    low = lane_low(q2.shape)
+
+    def pick(a, b):
+        return jnp.where(low, a, b)
+
+    ds0 = jnp.where(keep, dot_t(e0, g0), 0.0).astype(BF)
+    ds1 = jnp.where(keep, dot_t(e1, g1), 0.0).astype(BF)
+    dfq = pick(dot(ds0, k2), dot(ds1, k2)) + dot_t(jnp.concatenate([e0, e1], axis=1), split_state(st))
+    dq[rows, c] = (dfq * jnp.minimum(q2.astype(F32), 1.0)).astype(BF)
+    dt0 = jnp.where(keep_t, dot_t(g0, e0), 0.0).astype(BF)
+    dt1 = jnp.where(keep_t, dot_t(g1, e1), 0.0).astype(BF)
+    dfk = pick(dot(dt0, q2), dot(dt1, q2)) + dot_t(jnp.concatenate([g0, g1], axis=1), split_state(dst))
+    dk[rows, c] = (dfk * jnp.minimum(k2.astype(F32), 1.0)).astype(BF)
+    st0, st1 = masked_scores(k2, q2, keep_t)
+    own = jnp.where(row_low((128, 128)) == lane_low((128, 128)), dst, jnp.zeros_like(dst))
+    dv[rows, c] = (pick(dot(st0, e0), dot(st1, e1)) + dot(k2, own)).astype(BF)
+
+
+def gelu_parts(s):
+    c0 = math.sqrt(2.0 / math.pi)
+    s2 = s * s
+    th = jnp.tanh(c0 * (s + 0.044715 * s * s2))
+    h = 0.5 * (1.0 + th)
+    slope = h + 0.5 * s * (1.0 - th * th) * (c0 * (1.0 + 3 * 0.044715 * s2))
+    return s * h, slope
+
+
+def loop_pairs(n, body):
+    def step(p, _):
+        body(p)
+        return 0
+
+    lax.fori_loop(0, n, step, 0)
+
+
+def front_kernel(nb, cflag, x, wg, gain, bias, pad, fq, fk, vb, inc, msg, a1):
+    t, d = x.shape
+    blk = t // nb
+    norm_forward(x, gain, bias, a1)
+    for g in range(wg.shape[0]):
+        project(a1, wg, g, pad, fq, fk, vb)
+    pg = msg.shape[1] // 128
+
+    def pair(p):
+        chunk_sums(p, blk, nb, fk, vb, inc)
+        cur = inc[0, p]
+        for n in range(1, nb):
+            cur = cflag[n] * cur + inc[n, p]
+        msg[p // pg, pl.ds(pl.multiple_of(lax.rem(p, pg) * 128, 128), 128), :] = cur.astype(BF)
+
+    loop_pairs(d // 128, pair)
+
+
+def middle_kernel(nb, cflag, sin, inc, fq, fk, vb, x, wot, gain, bias, att, rden, states, mid, a2):
+    t, d = x.shape
+    blk = t // nb
+    pg = sin.shape[1] // 128
+
+    def pair(p):
+        cur = sin[p // pg, pl.ds(pl.multiple_of(lax.rem(p, pg) * 128, 128), 128), :].astype(F32)
+        for n in range(nb):
+            used = cflag[n] * cur
+            st = used.astype(BF)
+            states[n, p] = st
+            cur = used + inc[n, p]
+            r0, r1 = attend(p, n, blk, fq, fk, vb, st)
+            attend_store(p, n, blk, r0, r1, att, rden)
+
+    loop_pairs(d // 128, pair)
+    ew = wot.shape[2]
+    mid[...] = x[...].astype(F32)
+    for g in range(wot.shape[0]):
+        mid[...] += dot_t(att[:, g * ew : (g + 1) * ew], wot[g])
+    norm_forward(mid, gain, bias, a2)
+
+
+def ffn_kernel(ns, mid, a2, co, wu, wd, lo, da2, gu, gd, a2t, cot, acc, wub, wdb, gub, gdb, isem, osem):
+    nz, d, ff = wu.shape
+    tile = wub.shape[2]
+    per = ff // tile
+    steps = nz * per
+
+    def fetch(i, slot):
+        g, j = i // per, lax.rem(i, per)
+        c = pl.ds(pl.multiple_of(j * tile, 128), tile)
+        return (
+            pltpu.make_async_copy(wu.at[g, :, c], wub.at[slot], isem.at[slot, 0]),
+            pltpu.make_async_copy(wd.at[g, c, :], wdb.at[slot], isem.at[slot, 1]),
+        )
+
+    def flush(i, slot):
+        g, j = i // per, lax.rem(i, per)
+        c = pl.ds(pl.multiple_of(j * tile, 128), tile)
+        return (
+            pltpu.make_async_copy(gub.at[slot], gu.at[g, :, c], osem.at[slot, 0]),
+            pltpu.make_async_copy(gdb.at[slot], gd.at[g, :, c], osem.at[slot, 1]),
+        )
+
+    for cp in fetch(0, 0):
+        cp.start()
+    transpose_perm(ns, a2, a2t)
+    transpose_perm(ns, co, cot)
+    acc[...] = mid[...]
+    da2[...] = jnp.zeros_like(da2)
+
+    def step(i, _):
+        slot = lax.rem(i, 2)
+
+        @pl.when(i + 1 < steps)
+        def _():
+            for cp in fetch(i + 1, 1 - slot):
+                cp.start()
+
+        for cp in fetch(i, slot):
+            cp.wait()
+
+        @pl.when(i >= 2)
+        def _():
+            for cp in flush(i - 2, slot):
+                cp.wait()
+
+        up = dot(a2[...], wub[slot])
+        hidf, slope = gelu_parts(up)
+        hid = hidf.astype(BF)
+        acc[...] += dot(hid, wdb[slot])
+        gdb[slot] = dot(cot[...], hid).astype(BF)
+        dup = (slope * dot_t(co[...], wdb[slot])).astype(BF)
+        da2[...] += dot_t(dup, wub[slot])
+        gub[slot] = dot(a2t[...], dup).astype(BF)
+        for cp in flush(i, slot):
+            cp.start()
+        return 0
+
+    lax.fori_loop(0, steps, step, 0)
+    for i in range(max(0, steps - 2), steps):
+        for cp in flush(i, i % 2):
+            cp.wait()
+    lo[...] = acc[...].astype(BF)
+
+
+def turn_kernel(nb, cflag, da2, mid, co, gain, wot, fq, att, rden, dmid, dml, dr0, dr1, ginc, msg, sums, datt):
+    t, d = mid.shape
+    blk = t // nb
+    pg = msg.shape[1] // 128
+
+    def emit(rows, v):
+        dmid[rows, :] = v
+        dml[rows, :] = v.astype(BF)
+
+    norm_backward(da2, mid, gain, co, emit, sums)
+    ew = wot.shape[2]
+    for g in range(wot.shape[0]):
+        datt[:, g * ew : (g + 1) * ew] = dot(dml[...], wot[g])
+
+    def pair(p):
+        for n in range(nb):
+            attend_gradient(p, n, blk, datt, att, rden, dr0, dr1)
+        chunk_gradients(p, blk, nb, fq, dr0, dr1, ginc)
+        cur = cflag[nb - 1] * ginc[nb - 1, p]
+        for n in range(nb - 2, -1, -1):
+            cur = cflag[n] * (cur + ginc[n, p])
+        msg[p // pg, pl.ds(pl.multiple_of(lax.rem(p, pg) * 128, 128), 128), :] = cur.astype(BF)
+
+    loop_pairs(d // 128, pair)
+
+
+def back_kernel(nb, cflag, gin, ginc, states, fq, fk, vb, dr0, dr1, dq, dk, dv):
+    t, d = fq.shape
+    blk = t // nb
+    pg = gin.shape[1] // 128
+
+    def pair(p):
+        cur = gin[p // pg, pl.ds(pl.multiple_of(lax.rem(p, pg) * 128, 128), 128), :].astype(F32)
+        for n in range(nb - 1, -1, -1):
+            attend_backward(p, n, blk, fq, fk, vb, dr0, dr1, states[n, p], cur.astype(BF), dq, dk, dv)
+            cur = cflag[n] * (cur + ginc[n, p])
+
+    loop_pairs(d // 128, pair)
+
+
+def last_kernel(ns, x, gain, bias, dmid, dml, att, dq, dk, dv, wg, gt, g4, sums, a1, a1t, dmt, da1):
+    nz, _, d, ew = wg.shape
+    norm_forward(x, gain, bias, a1)
+    transpose_perm(ns, a1, a1t)
+    transpose_perm(ns, dml, dmt)
+    for g in range(nz):
+        c = slice(g * ew, (g + 1) * ew)
+        for k, r in enumerate((dq, dk, dv)):
+            g4[g, k] = dot(a1t[...], r[:, c]).astype(BF)
+            if g == 0 and k == 0:
+                da1[...] = dot_t(r[:, c], wg[g, k])
+            else:
+                da1[...] += dot_t(r[:, c], wg[g, k])
+        g4[g, 3] = dot(dmt[...], att[:, c]).astype(BF)
+
+    def emit(rows, v):
+        gt[rows, :] = v.astype(BF)
+
+    norm_backward(da1, x, gain, dmid, emit, sums)
+
+
+def on_core(name, kernel, outs, scratch, *args, hbm=(), smem=(), hbm_out=()):
+    ins = [any_spec() if i in hbm else smem_spec() if i in smem else vmem_spec() for i in range(len(args))]
+    return pl.pallas_call(
+        kernel,
+        out_shape=tuple(jax.ShapeDtypeStruct(s, dt) for s, dt in outs),
+        in_specs=ins,
+        out_specs=tuple(any_spec() if i in hbm_out else vmem_spec() for i in range(len(outs))),
+        scratch_shapes=scratch,
+        name=name,
+        compiler_params=pltpu.CompilerParams(vmem_limit_bytes=58 * 2**20),
+    )(*args)
+
+
+def group_order(nz):
+    out = []
+    for h in range(nz):
+        seq = [h]
+        for k in range(nz - 1):
+            for o in (h - 1 - k, h + 1 + k):
+                if 0 <= o < nz:
+                    seq.append(o)
+        out.append(seq)
+    return out
+
+
+def pick_group(order, h, i):
+    out = 0
+    for hh, seq in enumerate(order):
+        for ii, g in enumerate(seq):
+            if isinstance(i, int):
+                if ii == i:
+                    out = out + jnp.where(h == hh, g, 0)
+            else:
+                out = out + jnp.where((h == hh) & (i == ii), g, 0)
+    return out
+
+
+class Places:
+    def __init__(self, ns, nz):
+        self.ns, self.nz = ns, nz
+        self.s, self.h = lax.axis_index("seq"), lax.axis_index("head")
+        self.o0, self.o1 = bit_orders(ns)
+        self.m = ns.bit_length() - 1
+        self.zdev = z_others(self.s, self.h, nz)
+        self.zfrom = [(self.s, lax.rem(self.h + nz - 1 - d, nz)) for d in range(nz - 1)]
+        self.sdev = [(jnp.bitwise_xor(self.s, d), self.h) for d in range(1, ns)]
+        self.bit = [(jnp.bitwise_xor(self.s, 1 << b), self.h) for b in range(self.m)]
+        self.left, self.right = (self.s, self.h - 1), (self.s, self.h + 1)
+
+
+class Gather:
+    def __init__(self, pl_, buf, zs, zr, ps, pr, base):
+        self.p, self.buf, self.base = pl_, buf, base
+        self.sems = (zs, zr, ps, pr)
+        self.orders = (pl_.o0 + [0], pl_.o1 + [0])
+        self.half = buf.shape[2] // 2
+        self.r = self.half // pl_.ns
+        pos = [bits_to(pl_.s, o) for o in self.orders]
+        self.zrow = [f * self.half + pos[f] * self.r for f in range(2)]
+        self.mine = [
+            [f * self.half + ((pos[f] >> j) << j) * self.r for j in range(pl_.m)] for f in range(2)
+        ]
+        self.theirs = [
+            [f * self.half + jnp.bitwise_xor((pos[f] >> j) << j, 1 << j) * self.r for j in range(pl_.m)]
+            for f in range(2)
+        ]
+        h, nz = pl_.h, pl_.nz
+        self.origin = [(h - 1 - k, h + 1 + k) for k in range(nz - 1)]
+        self.valid = [(h - 1 - k >= 0, h + 1 + k < nz) for k in range(nz - 1)]
+        self.more = [((h - 1 - k >= 0) & (h + 1 < nz), (h + 1 + k < nz) & (h >= 1)) for k in range(nz - 1)]
+
+    def rows(self, start, n):
+        return pl.ds(pl.multiple_of(start, 16), n)
+
+    def zcopy(self, f, k, d, origin):
+        ref = self.buf.at[origin, :, self.rows(self.zrow[f], self.r), :]
+        i = ((self.base * 2 + f) * (self.p.nz - 1) + k) * 2 + d
+        return rcopy(ref, ref, self.sems[0].at[i], self.sems[1].at[i], self.p.right if d == 0 else self.p.left)
+
+    def pcopy(self, f, k, d, j, starts):
+        n = self.r << j
+        ref = self.buf.at[self.origin[k][d], :, self.rows(starts[f][j], n), :]
+        i = (((self.base * 2 + f) * (self.p.nz - 1) + k) * 2 + d) * self.p.m + j
+        return rcopy(ref, ref, self.sems[2].at[i], self.sems[3].at[i], self.p.bit[self.orders[f][j]])
+
+    def begin(self):
+        for d, cond in enumerate((self.p.h + 1 < self.p.nz, self.p.h >= 1)):
+
+            @pl.when(cond)
+            def _(d=d):
+                for f in range(2):
+                    self.zcopy(f, 0, d, self.p.h).start()
+
+    def advance(self, k, st):
+        for d in range(2):
+
+            @pl.when(self.valid[k][d])
+            def _(d=d):
+                for f in range(2):
+                    if st == 0:
+                        self.zcopy(f, k, d, self.origin[k][d]).wait_recv()
+                    else:
+                        self.pcopy(f, k, d, st - 1, self.theirs).wait_recv()
+                if st == 0 and k + 1 < self.p.nz - 1:
+
+                    @pl.when(self.more[k][d])
+                    def _():
+                        for f in range(2):
+                            self.zcopy(f, k + 1, d, self.origin[k][d]).start()
+
+                if st < self.p.m:
+                    for f in range(2):
+                        self.pcopy(f, k, d, st, self.mine).start()
+
+    def drain(self):
+        for d, cond in enumerate((self.p.h + 1 < self.p.nz, self.p.h >= 1)):
+
+            @pl.when(cond)
+            def _(d=d):
+                for f in range(2):
+                    self.zcopy(f, 0, d, self.p.h).wait_send()
+
+        for k in range(self.p.nz - 1):
+            for d in range(2):
+
+                @pl.when(self.valid[k][d])
+                def _(d=d, k=k):
+                    for f in range(2):
+                        for j in range(self.p.m):
+                            self.pcopy(f, k, d, j, self.mine).wait_send()
+                    if k + 1 < self.p.nz - 1:
+
+                        @pl.when(self.more[k][d])
+                        def _():
+                            for f in range(2):
+                                self.zcopy(f, k + 1, d, self.origin[k][d]).wait_send()
+
+
+class RowsIn:
+    def __init__(self, pl_, src, dst, ssem, rsem, lsem, base):
+        self.p, self.src, self.dst, self.sems, self.base = pl_, src, dst, (ssem, rsem, lsem), base
+        self.t, self.ew = dst.shape[0], src.shape[1]
+
+    def copy(self, d, dev, col):
+        i = self.base * (self.p.nz - 1) + d
+        return rcopy(
+            self.src.at[pl.ds(pl.multiple_of(dev[1] * self.t, 16), self.t), :],
+            self.dst.at[:, pl.ds(pl.multiple_of(col * self.ew, 128), self.ew)],
+            self.sems[0].at[i],
+            self.sems[1].at[i],
+            dev,
+        )
+
+    def own(self):
+        h = self.p.h
+        return pltpu.make_async_copy(
+            self.src.at[pl.ds(pl.multiple_of(h * self.t, 16), self.t), :],
+            self.dst.at[:, pl.ds(pl.multiple_of(h * self.ew, 128), self.ew)],
+            self.sems[2].at[self.base],
+        )
+
+    def begin(self):
+        for d, dev in enumerate(self.p.zdev):
+            self.copy(d, dev, self.p.h).start()
+        self.own().start()
+
+    def finish(self):
+        for d, frm in enumerate(self.p.zfrom):
+            self.copy(d, frm, frm[1]).wait_recv()
+        self.own().wait()
+
+    def drain(self):
+        for d, dev in enumerate(self.p.zdev):
+            self.copy(d, dev, self.p.h).wait_send()
+
+
+class Scan:
+    def __init__(self, pl_, wt, wp, wl, msg, r1, r2, tot, outb, got, sems):
+        self.p, self.w, self.msg, self.r1, self.r2 = pl_, (wt, wp, wl), msg, r1, r2
+        self.tot, self.outb, self.got, self.sems = tot, outb, got, sems
+
+    def c1(self, d, dev, slot):
+        return rcopy(self.msg.at[dev[1]], self.r1.at[slot], self.sems[0].at[d], self.sems[1].at[d], dev)
+
+    def c2(self, d, dev, slot):
+        return rcopy(self.tot, self.r2.at[slot], self.sems[2].at[d], self.sems[3].at[d], dev)
+
+    def c3(self, d, dev, slot):
+        return rcopy(self.outb.at[dev[1]], self.got.at[slot], self.sems[4].at[d], self.sems[5].at[d], dev)
+
+    def phase1(self):
+        for d, dev in enumerate(self.p.zdev):
+            self.c1(d, dev, self.p.h).start()
+        self.r1[self.p.h] = self.msg[self.p.h]
+
+    def phase2(self):
+        for d, frm in enumerate(self.p.zfrom):
+            self.c1(d, frm, frm[1]).wait_recv()
+        wt = self.w[0]
+        self.tot[...] = sum(wt[z] * self.r1[z].astype(F32) for z in range(self.p.nz)).astype(BF)
+        for d, dev in enumerate(self.p.sdev):
+            self.c2(d, dev, self.p.s).start()
+        self.r2[self.p.s] = self.tot[...]
+
+    def phase3(self):
+        for d, dev in enumerate(self.p.sdev):
+            self.c2(d, dev, dev[0]).wait_recv()
+        _, wp, wl = self.w
+        for z in range(self.p.nz):
+            v = sum(wl[z, k] * self.r1[k].astype(F32) for k in range(self.p.nz))
+            v = v + sum(wp[z, k] * self.r2[k].astype(F32) for k in range(self.p.ns))
+            self.outb[z] = v.astype(BF)
+        for d, dev in enumerate(self.p.zdev):
+            self.c3(d, dev, self.p.h).start()
+        self.got[self.p.h] = self.outb[self.p.h]
+
+    def finish(self):
+        for d, frm in enumerate(self.p.zfrom):
+            self.c3(d, frm, frm[1]).wait_recv()
+
+    def drain(self):
+        for d, dev in enumerate(self.p.zdev):
+            self.c1(d, dev, self.p.h).wait_send()
+            self.c3(d, dev, self.p.h).wait_send()
+        for d, dev in enumerate(self.p.sdev):
+            self.c2(d, dev, self.p.s).wait_send()
+
+
+def state_part(p, n, blk, fq, vals, st):
+    rows = pl.ds(n * blk, blk)
+    r = dot(fq[rows, cols(p, 128)], split_state(st))
+    low = lane_low((blk, 128))
+    num = jnp.where(low, r[:, :128], r[:, 128:])
+    den = pltpu.roll(jnp.where(low, r[:, 128:], r[:, :128]), HD, 1)
+    return num, den
+
+
+def fore_kernel(ns, nz, nb, *refs):
+    cflag, wt, wp, wl = refs[:4]
+    tok, cot, wq, wo, wu, wd, gains, biases, pad = refs[4:13]
+    xo, coo, fqo, fko, vbo, atto, rdeno, stateso, mido, w4o, lo, da2o, gu, gd = refs[13:27]
+    (xv, cov, av, fq, fk, vb, att, a2t, ct, rden, mid, acc, da2, inc, states,
+     w4v, wuv, wdv, gub, gdb, msg, r1, r2, tot, outb, got,
+     lsem, tsend, trecv, zsend, zrecv, psend, precv, wsem, ysem, osem,
+     c1s, c1r, c2s, c2r, c3s, c3r) = refs[27:]
+    P_ = Places(ns, nz)
+    t, d = xv.shape
+    blk = t // nb
+    ew = wq.shape[2]
+    ff = wu.shape[2]
+    h = P_.h
+    m = P_.m
+    np_ = d // 128
+    pg = msg.shape[1] // 128
+    order = group_order(nz)
+    gidx = [pick_group(order, h, i) for i in range(nz)]
+    W = Gather(P_, w4v, zsend, zrecv, psend, precv, 0)
+    U = Gather(P_, wuv, zsend, zrecv, psend, precv, 1)
+    V = Gather(P_, wdv, zsend, zrecv, psend, precv, 2)
+    X = RowsIn(P_, tok, xv, tsend, trecv, lsem, 0)
+    C = RowsIn(P_, cot, cov, tsend, trecv, lsem, 1)
+    scan = Scan(P_, wt, wp, wl, msg, r1, r2, tot, outb, got, (c1s, c1r, c2s, c2r, c3s, c3r))
+    own = [
+        pltpu.make_async_copy(wq, w4v.at[h, 0:3], wsem.at[0]),
+        pltpu.make_async_copy(wo, w4v.at[h, 3:4], wsem.at[1]),
+        pltpu.make_async_copy(wu, wuv.at[h], wsem.at[2]),
+        pltpu.make_async_copy(wd, wdv.at[h], wsem.at[3]),
+    ]
+    for cp in own:
+        cp.start()
+    enter(P_.zdev + P_.sdev)
+    X.begin()
+    own[0].wait()
+    own[1].wait()
+    W.begin()
+    outs = []
+
+    def keep(src, dst):
+        cp = pltpu.make_async_copy(src, dst, ysem.at[len(outs)])
+        outs.append(cp)
+        cp.start()
+
+    parts = [(a, k) for k in range(nz - 1) for a in (U, V)]
+    waves = []
+    for w in range(len(parts) - 1 + 2 * m + 1):
+        waves.append([(a, k, (w - i) // 2) for i, (a, k) in enumerate(parts) if 0 <= w - i <= 2 * m and (w - i) % 2 == 0])
+    done_at = [len(parts[: 2 * k + 2]) - 1 + 2 * m for k in range(nz - 1)]
+    state = {"w": 0}
+
+    def tick(upto=None):
+        upto = state["w"] if upto is None else upto
+        while state["w"] <= upto and state["w"] < len(waves):
+            for a, k, st in waves[state["w"]]:
+                a.advance(k, st)
+            state["w"] += 1
+
+    W.advance(0, 0)
+    X.finish()
+    own[2].wait()
+    own[3].wait()
+    U.begin()
+    V.begin()
+    norm_forward(xv, gains.at[0:1], biases.at[0:1], av)
+    keep(xv, xo)
+    project(av, w4v, gidx[0], pad, fq, fk, vb)
+    for w in range(1, nz - 1 + m):
+        for k in range(nz - 1):
+            if 0 <= w - k <= m:
+                W.advance(k, w - k)
+                if w - k == m:
+                    project(av, w4v, gidx[k + 1], pad, fq, fk, vb)
+        if w == nz - 2:
+            C.begin()
+    keep(w4v, w4o)
+    keep(fq, fqo)
+    keep(fk, fko)
+    keep(vb, vbo)
+    tick()
+
+    def sums_of(p):
+        chunk_sums(p, blk, nb, fk, vb, inc)
+        cur = inc[0, p]
+        for n in range(1, nb):
+            cur = cflag[n] * cur + inc[n, p]
+        msg[p // pg, pl.ds(pl.multiple_of(lax.rem(p, pg) * 128, 128), 128), :] = cur.astype(BF)
+
+    loop_pairs(np_, sums_of)
+    scan.phase1()
+    tick()
+
+    def local_of(p):
+        for n in range(nb):
+            rows = pl.ds(n * blk, blk)
+            c = cols(p, 128)
+            q2, k2, v2 = fq[rows, c], fk[rows, c], vb[rows, c]
+            s0, s1 = masked_scores(q2, k2, causal_mask(blk))
+            g0, g1 = with_ones(v2)
+            x0, x1 = dot(s0, g0), dot(s1, g1)
+            low = lane_low(x0.shape)
+            acc[rows, c] = jnp.where(low, x0, x1)
+            rden[rows, c] = pltpu.roll(jnp.where(low, x1, x0), HD, 1)
+
+    hp = np_ // 2
+    loop_pairs(hp, local_of)
+    scan.phase2()
+    tick()
+    loop_pairs(np_ - hp, lambda p: local_of(p + hp))
+    scan.phase3()
+    tick()
+    scan.finish()
+
+    def state_of(p):
+        cur = got[p // pg, pl.ds(pl.multiple_of(lax.rem(p, pg) * 128, 128), 128), :].astype(F32)
+        for n in range(nb):
+            rows = pl.ds(n * blk, blk)
+            c = cols(p, 128)
+            used = cflag[n] * cur
+            st = used.astype(BF)
+            states[n, p] = st
+            cur = used + inc[n, p]
+            num, den = state_part(p, n, blk, fq, None, st)
+            rd = 1.0 / (1.0 + rden[rows, c] + den)
+            att[rows, c] = ((acc[rows, c] + num) * rd).astype(BF)
+            rden[rows, c] = rd
+
+    loop_pairs(np_, state_of)
+    keep(att, atto)
+    keep(rden, rdeno)
+    keep(states, stateso)
+    tick()
+    mid[...] = xv[...].astype(F32)
+    for g in range(nz):
+        mid[...] += dot_t(att[:, g * ew : (g + 1) * ew], w4v[g, 3])
+        if g % 2 == 1:
+            tick()
+    norm_forward(mid, gains.at[1:2], biases.at[1:2], av)
+    keep(mid, mido)
+    C.finish()
+    keep(cov, coo)
+    transpose_perm(ns, av, a2t)
+    transpose_perm(ns, cov, ct)
+    acc[...] = mid[...]
+    da2[...] = jnp.zeros_like(da2)
+    tile = gub.shape[2]
+    per = ff // tile
+    steps = nz * per
+
+    def place(i):
+        g = pick_group(order, h, i // per)
+        return g, pl.ds(pl.multiple_of(lax.rem(i, per) * tile, 128), tile)
+
+    def flush(i, slot):
+        g, c = place(i)
+        return (
+            pltpu.make_async_copy(gub.at[slot], gu.at[g, :, c], osem.at[slot, 0]),
+            pltpu.make_async_copy(gdb.at[slot], gd.at[g, :, c], osem.at[slot, 1]),
+        )
+
+    def step(i, _):
+        slot = lax.rem(i, 2)
+        for k in range(nz - 1):
+
+            @pl.when(i == (k + 1) * per)
+            def _(k=k):
+                tick(done_at[k])
+
+        @pl.when(i >= 2)
+        def _():
+            for cp in flush(i - 2, slot):
+                cp.wait()
+
+        g, c = place(i)
+        wub, wdb = wuv[g, 0, :, c], wdv[g, 0, c, :]
+        up = dot(av[...], wub)
+        hidf, slope = gelu_parts(up)
+        hid = hidf.astype(BF)
+        acc[...] += dot(hid, wdb)
+        gdb[slot] = dot(ct[...], hid).astype(BF)
+        dup = (slope * dot_t(cov[...], wdb)).astype(BF)
+        da2[...] += dot_t(dup, wub)
+        gub[slot] = dot(a2t[...], dup).astype(BF)
+        for cp in flush(i, slot):
+            cp.start()
+        return 0
+
+    lax.fori_loop(0, steps, step, 0)
+    tick(len(waves))
+    keep(da2, da2o)
+    av[...] = acc[...].astype(BF)
+    keep(av, lo)
+    for i in range(max(0, steps - 2), steps):
+        for cp in flush(i, i % 2):
+            cp.wait()
+    for cp in outs:
+        cp.wait()
+    X.drain()
+    C.drain()
+    scan.drain()
+    for a in (W, U, V):
+        a.drain()
+
+
+def fore(ns, nz, nb, tables, tok, cot, wq, wo, wu, wd, gains, biases, pad):
+    t, d = tok.shape[0] // nz, wq.shape[1]
+    ew, ff = wq.shape[2], wu.shape[2]
+    np_ = d // 128
+    m = ns.bit_length() - 1
+    dma = pltpu.SemaphoreType.DMA
+    vm = pltpu.VMEM
+    tile = 512 if ff % 512 == 0 else ff
+    one = ((ew // 128) * 128, 128)
+    nzs = 3 * 2 * (nz - 1) * 2
+    td, tdf = ((t, d), BF), ((t, d), F32)
+    outs = [td, td, td, td, td, td, tdf, ((nb, np_, 128, 128), BF), tdf, ((nz, 4, d, ew), BF), td, tdf,
+            ((nz, d, ff), BF), ((nz, d, ff), BF)]
+    args = tables + (tok, cot, wq, wo, wu, wd, gains, biases, pad)
+    return pl.pallas_call(
+        functools.partial(fore_kernel, ns, nz, nb),
+        out_shape=tuple(jax.ShapeDtypeStruct(s, dt) for s, dt in outs),
+        in_specs=[smem_spec()] * 4 + [any_spec()] * 6 + [vmem_spec()] * 3,
+        out_specs=(any_spec(),) * len(outs),
+        scratch_shapes=[vm((t, d), BF)] * 7
+        + [vm((d, t), BF)] * 2
+        + [vm((t, d), F32)] * 4
+        + [
+            vm((nb, np_, 128, 128), F32),
+            vm((nb, np_, 128, 128), BF),
+            vm((nz, 4, d, ew), BF),
+            vm((nz, 1, d, ff), BF),
+            vm((nz, 1, ff, d), BF),
+            vm((2, d, tile), BF),
+            vm((2, d, tile), BF),
+            vm((nz,) + one, BF),
+            vm((nz,) + one, BF),
+            vm((ns,) + one, BF),
+            vm(one, BF),
+            vm((nz,) + one, BF),
+            vm((nz,) + one, BF),
+            dma((2,)),
+            dma((2 * (nz - 1),)),
+            dma((2 * (nz - 1),)),
+            dma((nzs,)),
+            dma((nzs,)),
+            dma((nzs * m,)),
+            dma((nzs * m,)),
+            dma((4,)),
+            dma((16,)),
+            dma((2, 2)),
+        ]
+        + [dma((nz - 1,)), dma((nz - 1,)), dma((ns - 1,)), dma((ns - 1,)), dma((nz - 1,)), dma((nz - 1,))],
+        name="fore",
+        compiler_params=pltpu.CompilerParams(collective_id=0, has_side_effects=True, vmem_limit_bytes=62 * 2**20),
+    )(*args)
 
 
 def shards(ns, nz, tokens, lengths, pad_mask, w_qkv, w_out, w_up, w_down, norm_gains, norm_biases, out_cotangent):
     rows = tokens.shape[0]
     t = rows // nz
     d = w_qkv.shape[1]
-    nh = d // HD
-    gh = nh // nz
+    ff = w_up.shape[1]
     ew = d // nz
+    np_ = d // 128
     blk = math.gcd(t, UNIT)
     nb = t // blk
     s, h = lax.axis_index("seq"), lax.axis_index("head")
@@ -557,124 +1428,51 @@
     bwp = ((sidx[None, :] > s) & (before2[None, :, 0] == my_last[:, None])).astype(F32)
     bwl = ((zidx[None, :] > zidx[:, None]) & (my_before[None, :] == my_last[:, None])).astype(F32)
 
-    w4 = jnp.concatenate([w_qkv, w_out.T[None]], axis=0)
-    x, co, w4g, wug, wdg = gather_all(ns, nz, tokens, out_cotangent, w4, w_up[None], w_down[None])
-    wug, wdg = wug[:, 0], wdg[:, 0]
     pad = lax.dynamic_slice_in_dim(pad_mask, h * t, t).astype(F32)[:, None]
-    xf = x.astype(F32)
-    a1f, pull1 = jax.vjp(layer_norm, xf, norm_gains[0], norm_biases[0])
-    a1 = a1f.astype(BF)
-    qkv = dot("td,hcde->cthe", a1, w4g[:, :3]).reshape(3, t, d)
-    q, k = qkv[0], qkv[1]
-    fq = jnp.where(q > 0, q + 1.0, jnp.exp(jnp.minimum(q, 0.0))).astype(BF)
-    fk = (pad * jnp.where(k > 0, k + 1.0, jnp.exp(jnp.minimum(k, 0.0)))).astype(BF)
-    vb = qkv[2].astype(BF)
-
-    def heads(a):
-        return a.reshape(nb, blk, nh, HD)
-
-    fqh, fkh, vbh = heads(fq), heads(fk), heads(vb)
-    inc = dot("nuhk,nuhv->nhkv", fkh, vbh)
-    zinc = jnp.sum(fkh.astype(F32), axis=1)
-
-    def pack(state, norm):
-        m1 = state.reshape(nz, gh, HD, HD).transpose(0, 2, 1, 3).reshape(nz, HD, ew)
-        m2 = jnp.pad(norm.reshape(nz, 1, ew), ((0, 0), (0, MSG - HD - 1), (0, 0)))
-        return jnp.concatenate([m1, m2], axis=1).astype(BF)
-
-    def unpack(msg):
-        msg = msg.astype(F32)
-        st = msg[:, :HD].reshape(nz, HD, gh, HD).transpose(0, 2, 1, 3).reshape(nh, HD, HD)
-        return st, msg[:, HD].reshape(nh, HD)
-
-    sl, zl = inc[0], zinc[0]
-    for n in range(1, nb):
-        sl, zl = cflag[n] * sl + inc[n], cflag[n] * zl + zinc[n]
-    st, zt = unpack(scan_states(ns, nz, 1, fwt, fwp, fwl, pack(sl, zl)))
-    states, norms = [], []
-    for n in range(nb):
-        states.append(cflag[n] * st)
-        norms.append(cflag[n] * zt)
-        st, zt = cflag[n] * st + inc[n], cflag[n] * zt + zinc[n]
-    states = jnp.stack(states).astype(BF)
-    norms = jnp.stack(norms)
-    causal = (jnp.arange(blk)[:, None] >= jnp.arange(blk)[None, :]).astype(F32)
-    scores = (causal * dot("nthk,nuhk->nhtu", fqh, fkh)).astype(BF)
-    numer = dot("nhtu,nuhv->nthv", scores, vbh) + dot("nthk,nhkv->nthv", fqh, states)
-    ks = dot("tu,nuhk->nthk", causal.astype(BF), fkh) + norms[:, None]
-    den = 1.0 + jnp.sum(fqh.astype(F32) * ks, axis=-1)
-    att = (numer / den[..., None]).reshape(t, d).astype(BF)
+    gains = [norm_gains[i : i + 1] for i in range(2)]
+    biases = [norm_biases[i : i + 1] for i in range(2)]
+    td, tdf = ((t, d), BF), ((t, d), F32)
+    msgs = ((nz, (ew // 128) * 128, 128), BF)
+    incs = ((nb, np_, 128, 128), F32)
+    sums = ((2, 8, d), F32)
+    vm = pltpu.VMEM
+    x, co, fq, fk, vb, att, rden, states, mid, w4g, lo, da2, gu, gd = fore(
+        ns, nz, nb, (cflag, fwt, fwp, fwl), tokens, out_cotangent, w_qkv, w_out.T[None], w_up[None], w_down[None],
+        norm_gains, norm_biases, pad,
+    )
     wot = w4g[:, 3]
-    mid = xf + dot("the,hde->td", att.reshape(t, nz, ew), wot)
-    a2f, pull2 = jax.vjp(layer_norm, mid, norm_gains[1], norm_biases[1])
-    a2 = a2f.astype(BF)
-    up = dot("td,hdf->thf", a2, wug)
-    gel, pullg = jax.vjp(jax.nn.gelu, up)
-    hid = gel.astype(BF)
-    lo = (mid + dot("thf,hfd->td", hid, wdg)).astype(BF)
-    d_up = pullg(dot("td,hfd->thf", co, wdg))[0].astype(BF)
-    d_a2 = dot("thf,hdf->td", d_up, wug)
-    d_mid_n, gain2, bias2 = pull2(d_a2)
-    d_mid = co.astype(F32) + d_mid_n
-    dml = d_mid.astype(BF)
-    d_att = dot("td,hde->the", dml, wot).reshape(nb, blk, nh, HD)
-    d_num = (d_att / den[..., None]).astype(BF)
-    d_den = -jnp.sum(d_att * numer, axis=-1) / (den * den)
-    d_ks = d_den[..., None] * fqh.astype(F32)
-    gloc = dot("nthk,nthv->nhkv", fqh, d_num)
-    yloc = jnp.sum(d_ks, axis=1)
-    sl, zl = cflag[nb - 1] * gloc[nb - 1], cflag[nb - 1] * yloc[nb - 1]
-    for n in range(nb - 2, -1, -1):
-        sl, zl = cflag[n] * (sl + gloc[n]), cflag[n] * (zl + yloc[n])
-    st, zt = unpack(scan_states(ns, nz, 2, bwt, bwp, bwl, pack(sl, zl)))
-    d_inc, d_zinc = [None] * nb, [None] * nb
-    for n in range(nb - 1, -1, -1):
-        d_inc[n], d_zinc[n] = st, zt
-        st, zt = cflag[n] * (st + gloc[n]), cflag[n] * (zt + yloc[n])
-    d_inc = jnp.stack(d_inc).astype(BF)
-    d_zinc = jnp.stack(d_zinc)
-    d_scores = (causal * dot("nthv,nuhv->nhtu", d_num, vbh)).astype(BF)
-    d_fq = (
-        d_den[..., None] * ks
-        + dot("nthv,nhkv->nthk", d_num, states)
-        + dot("nhtu,nuhk->nthk", d_scores, fkh)
+    dmid, dml, dr0, dr1, ginc, gmsg, sums2 = on_core(
+        "turn",
+        functools.partial(turn_kernel, nb),
+        (tdf, td, td, td, incs, msgs, sums),
+        [vm((t, d), F32)],
+        cflag, da2, mid, co, gains[1], wot, fq, att, rden,
+        smem=(0,),
     )
-    d_fk = (
-        dot("tu,nthk->nuhk", causal.astype(BF), d_ks.astype(BF))
-        + dot("nhtu,nthk->nuhk", d_scores, fqh)
-        + dot("nuhv,nhkv->nuhk", vbh, d_inc)
-        + d_zinc[:, None]
+    gin = scan_states(ns, nz, 2, bwt, bwp, bwl, gmsg)
+    dq, dk, dv = on_core(
+        "back",
+        functools.partial(back_kernel, nb),
+        (td, td, td),
+        [],
+        cflag, gin, ginc, states, fq, fk, vb, dr0, dr1,
+        smem=(0,),
     )
-    d_v = dot("nhtu,nthv->nuhv", scores, d_num) + dot("nuhk,nhkv->nuhv", fkh, d_inc)
-    d_q = (d_fq.reshape(t, d) * jnp.where(q > 0, 1.0, jnp.exp(jnp.minimum(q, 0.0)))).astype(BF)
-    d_k = (d_fk.reshape(t, d) * pad * jnp.where(k > 0, 1.0, jnp.exp(jnp.minimum(k, 0.0)))).astype(BF)
-    d_qkv = jnp.stack([d_q, d_k, d_v.reshape(t, d).astype(BF)]).reshape(3, t, nz, ew)
-    d_a1 = dot("cthe,hcde->td", d_qkv, w4g[:, :3])
-    d_x, gain1, bias1 = pull1(d_a1)
-    gt = (d_mid + d_x).astype(BF)
-
-    o0, o1 = bit_orders(ns)
-    m = ns.bit_length() - 1
-
-    def perm(a):
-        u = d // (2 * ns)
-        a = a.reshape((t,) + (2,) * m + (2, u))
-        parts = []
-        for f, order in enumerate(([0] + o0, [0] + o1)):
-            v = a[..., f, :]
-            v = v.transpose((0,) + tuple(m - b for b in order) + (m + 1,))
-            parts.append(v.reshape(t, d // 2))
-        return jnp.concatenate(parts, axis=1)
-
-    a1p = perm(a1)
-    g_qkv = dot("td,cthe->hcde", a1p, d_qkv).astype(BF)
-    g_out = dot("td,the->hde", perm(dml), att.reshape(t, nz, ew)).astype(BF)
-    g4 = jnp.concatenate([g_qkv, g_out[:, None]], axis=1).reshape(nz, 4, 2, d // 2, ew)
-    ff = w_up.shape[1]
-    gu = dot("td,thf->hdf", perm(a2), d_up).astype(BF).reshape(nz, 1, 2, d // 2, ff)
-    gd = dot("td,thf->hdf", perm(co), hid).astype(BF).reshape(nz, 1, 2, d // 2, ff)
-    gb = jnp.concatenate([jnp.stack([gain1, gain2, bias1, bias2]), jnp.zeros((4, d), F32)])
-    lo_o, gt_o, gbo, o4, ou, od = reduce_all(ns, nz, lo, gt, gb, g4, gu, gd)
+    gt, g4, sums1 = on_core(
+        "last",
+        functools.partial(last_kernel, ns),
+        (td, ((nz, 4, d, ew), BF), sums),
+        [vm((t, d), BF), vm((d, t), BF), vm((d, t), BF), vm((t, d), F32)],
+        x, gains[0], biases[0], dmid, dml, att, dq, dk, dv, w4g,
+    )
+    s1, s2 = jnp.sum(sums1, axis=1), jnp.sum(sums2, axis=1)
+    gb = jnp.concatenate([jnp.stack([s1[0], s2[0], s1[1], s2[1]]), jnp.zeros((4, d), F32)])
+    lo_o, gt_o, gbo, o4, ou, od = reduce_all(
+        ns, nz, lo, gt, gb,
+        g4.reshape(nz, 4, 2, d // 2, ew),
+        gu.reshape(nz, 1, 2, d // 2, ff),
+        gd.reshape(nz, 1, 2, d // 2, ff),
+    )
     piece = d // ns
     o4 = o4.reshape(4, piece, ew).astype(F32)
     w = d // ndev

time: 779 us -> 475 us (0.61)
  matrix products: 145 us -> 0 us
  local copies, waits for them, and re-layouts: 137 us -> 15.1 us
  other arithmetic: 61.2 us -> 10.9 us
  Pallas kernels: 427 us -> 439 us
    dot_general x26 -> x0, matrix products: 145 us -> none  [dot(): return jnp.einsum(spec, a, b, preferred_element_type=F32)]
    convert_element_type x13 -> x0, local copies, waits for them, and re-layouts: 47.2 us -> none  [the longest x3 10.2 us: shards(): d_v.reshape(t, d).astype(BF)]
    reshape x15 -> x0, local copies, waits for them, and re-layouts: 28.3 us -> none  [the longest x2 9.39 us: shards(): d_fk.reshape(t, d) * pad]
    pallas_call x1 -> x4, Pallas kernels: 214 us -> 231 us  [the longest x1 170 us: fore(): pl.pallas_call(functools.partial(fore_kernel, ns, nz, nb), out_shape=tupl...]
    convert_element_type x9 -> x0, other arithmetic: 14.7 us -> none  [the longest x1 5.12 us: shards(): (d_fq.reshape(t, d) * jnp.where(q > 0, 1.0, jnp.exp(jnp.minimum(q, 0.0)))...]
    concatenate x4 -> x0, other arithmetic: 12 us -> none  [the longest x1 6.83 us: shards(): jnp.concatenate([g_qkv, g_out[:, None]], axis=1)]
    another operation x12 -> x2, other arithmetic: 11.2 us -> 0.16 us
    select_n x2 -> x0, local copies, waits for them, and re-layouts: 9.18 us -> none  [shards(): jnp.where(k > 0, k + 1.0, jnp.exp(jnp.minimum(k, 0.0)))]
where the time goes in v2:
time: 475 us; the launch traced here: 466 us
  Pallas kernels  439 us (92%)
  local copies, waits for them, and re-layouts  15.1 us (3%)
  other arithmetic  10.9 us (2%)
    pallas_call x1, Pallas kernels, reduce_all(): pl.pallas_call(functools.partial(reduce_kernel, ns, nz), out_shape=(jax.S...  175 us
    pallas_call x1, Pallas kernels, fore(): pl.pallas_call(functools.partial(fore_kernel, ns, nz, nb), out_shape=tupl...  170 us
    pallas_call x3, Pallas kernels, on_core(): pl.pallas_call(kernel, out_shape=tuple((jax.ShapeDtypeStruct(s, dt) for s...  61 us
    pallas_call x1, Pallas kernels, scan_states(): pl.pallas_call(functools.partial(scan_kernel, ns, nz), out_shape=jax.Shap...  33.4 us

profile of v2, /device:TPU:24, one launch (start us, length us, event | category | flops | bytes accessed | tf_op | source)
XLA Modules:
  0.0 466.2 jit_solution(1410330067679043212)
XLA Ops:
  0.6 0.7 copy.29
  1.4 0.1 reduce
  1.5 0.1 convert_reduce_fusion
  1.6 0.1 pad_add_fusion
  1.7 0.6 dynamic_slice.15
  2.3 0.2 convert_reduce_fusion.1
  2.5 1.2 compare_convert_fusion.2.refs_0_.cflag
  3.7 0.1 reshape.98
  3.8 0.1 reshape.97
  3.9 0.7 fusion.3
  4.6 0.6 slice.62
  5.1 1.2 compare_convert_fusion.1.refs_1_
  6.3 0.2 slice_reduce_fusion.1
  6.5 0.7 and_convert_fusion.1.refs_2_
  7.1 0.8 dynamic-slice_convert_fusion
  7.9 0.9 broadcast_in_dim.30.refs_12_
  8.8 2.0 copy.30
  10.8 169.6 %fore.1 = (bf16[576,1024]{1,0:T(8,128)(2,1)}, bf16[576,1024]{1,0:T(8,128)(2,1)}, bf16[576,1024]{1,0:T(8,128)(2,1)}, bf16[576,1024]{1,0:T(8,128)(2,1)}, bf16[576,...) custom-call(f32[3]{0:T(128)} %compare_convert_fusion.2.refs_0_.cflag, ...), custom_call_target="tpu_custom_call" | custom-call | tf_op jit(solution)/shard_map/fore/pallas_call | solution.py:1359
  180.4 0.0 copy-start.5
  180.4 3.1 slice_bitcast_fusion.wot
  183.5 0.0 copy-done.5
  183.5 0.6 fusion.6
  184.1 15.4 %turn.1 = (f32[576,1024]{1,0:T(8,128)}, bf16[576,1024]{1,0:T(8,128)(2,1)}, bf16[576,1024]{1,0:T(8,128)(2,1)}, bf16[576,1024]{1,0:T(8,128)(2,1)}, f32[3,8,128,128...) custom-call(f32[3]{0:T(128)} %compare_convert_fusion.2.refs_0_.cflag, ...), custom_call_target="tpu_custom_call" | custom-call | tf_op jit(solution)/shard_map/turn/pallas_call | solution.py:905
  199.5 0.5 compare_convert_fusion.wt
  200.1 0.1 slice_reduce_fusion
  200.2 0.7 and_convert_fusion.wp
  200.8 33.4 %scan_states.1.gin = bf16[4,256,128]{2,1,0:T(8,128)(2,1)} custom-call(f32[4]{0:T(128)} %compare_convert_fusion.wt, f32[4,8]{1,0:T(4,128)} %and_convert_fusion.wp, f32[4,4]{1,0:T(4,128)} %get-tuple-element.82.wl, bf16[4,256,128]{2,1,0:T(8,128)(2,1)} %get-tuple-element.52.msg), custom_call_target="tpu_custom_call" | custom-call | tf_op jit(solution)/shard_map/scan_states/pallas_call | solution.py:264
  234.3 0.0 copy-start.6
  234.3 21.5 %back.1 = (bf16[576,1024]{1,0:T(8,128)(2,1)}, bf16[576,1024]{1,0:T(8,128)(2,1)}, bf16[576,1024]{1,0:T(8,128)(2,1)}) custom-call(f32[3]{0:T(128)} %compare_convert_fusion.2.refs_0_.cflag, bf16[4,256,128]{2,1,0:T(8,128)(2,1)} %scan_states.1.gin, f32[3,8,128,128]{3,2,1,0:T(8,128)} %get-tuple-element.53.ginc, bf16[3,8,128,128]{3,2,1,0:T(8,128)(2,1)} %get-tuple-element.54.states, ...), custom_call_target="tpu_custom_call" | custom-call | tf_op jit(solution)/shard_map/back/pallas_call | solution.py:905
  255.8 0.0 copy-done.6
  255.8 0.6 slice.65.bias
  256.4 0.0 copy-start.4
  256.4 24.1 %last.1 = (bf16[576,1024]{1,0:T(8,128)(2,1)}, bf16[4,4,1024,256]{3,2,1,0:T(8,128)(2,1)}, f32[2,8,1024]{2,1,0:T(8,128)}) custom-call(bf16[576,1024]{1,0:T(8,128)(2,1)} %get-tuple-element.42.x, f32[1,1024]{1,0:T(1,128)} %get-tuple-element.79.gain, f32[1,1024]{1,0:T(1,128)} %slice.65.bias, f32[576,1024]{1,0:T(8,128)} %get-tuple-element.50.dmid, ...), custom_call_target="tpu_custom_call" | custom-call | tf_op jit(solution)/shard_map/last/pallas_call | solution.py:905
  280.5 0.9 reduce_sum.38
  281.4 0.0 copy-done.4
  281.4 0.7 concatenate.11.gb
  282.1 174.9 %reduce_all.1 = (bf16[2304,256]{1,0:T(8,128)(2,1)}, bf16[2304,256]{1,0:T(8,128)(2,1)}, f32[8,1024]{1,0:T(8,128)}, bf16[4,2,64,256]{3,2,1,0:T(8,128)(2,1)}, bf16[...) custom-call(bf16[576,1024]{1,0:T(8,128)(2,1)} %get-tuple-element.41.lo, ...), custom_call_target="tpu_custom_call" | custom-call | tf_op jit(solution)/shard_map/reduce_all/pallas_call | solution.py:480
  457.0 0.0 copy-start.3
  457.0 2.9 convert_element_type.57
  459.9 0.0 copy-start.2
  459.9 0.0 copy-start.1
  459.9 0.0 copy-done.3
  459.9 0.1 bitcast_convert_fusion
  460.0 0.0 copy-start
  460.0 1.0 copy.34
  461.0 0.0 copy-done.2
  461.0 0.9 bitcast_convert_fusion.1
  461.9 0.0 copy-done.1
  461.9 0.8 slice.84
  462.7 0.8 copy.33
  463.4 0.7 constant_dynamic-slice_fusion
  464.2 0.6 fusion.7
  464.8 0.0 copy-done
  464.8 1.0 copy.38
  (10 shorter events, 0.1 us)
Async XLA Ops:
  180.4 3.1 copy-start.5
  234.3 21.5 %copy-start.6 = (f32[2,1024]{1,0:T(2,128)S(1)}, f32[2,1024]{1,0:T(2,128)}, u32[]{:S(2)}) copy-start(f32[2,1024]{1,0:T(2,128)} %refs_11_.1) | copy-start | bytes 24580
  256.4 25.0 %copy-start.4 = (f32[2,8,1024]{2,1,0:T(8,128)S(1)}, f32[2,8,1024]{2,1,0:T(8,128)}, u32[]{:S(2)}) copy-start(f32[2,8,1024]{2,1,0:T(8,128)} %get-tuple-element.64) | copy-start | bytes 196612
  457.0 2.9 copy-start.3
  459.9 1.1 copy-start.2
  459.9 1.9 copy-start.1
  460.0 4.7 %copy-start = (bf16[2304,256]{1,0:T(8,128)(2,1)S(1)}, bf16[2304,256]{1,0:T(8,128)(2,1)}, u32[]{:S(2)}) copy-start(bf16[2304,256]{1,0:T(8,128)(2,1)} %get-tuple-element.96) | copy-start | bytes 3538948
